TPU v7x, 256 devices: a whole 4x4x8 slice. The times are simulated.
256 devices in a mesh: rep: 32 (over z_lo, x, y), fsdp: 8 (over z_hi, core).
Axes of the slice: x: 4, y: 4, z: 8 (z_hi: 4, z_lo: 2; z = z_hi * 2 + z_lo), core: 2. Of those that a mesh axis runs over, the one named last changes fastest.
Arguments:
- activations: bfloat16 [180224, 4096], P(('rep', 'fsdp')), may hold values from -6 to 6
- cotangent: bfloat16 [180224, 512], P(('rep', 'fsdp')), may hold values from -0.078125 to 0.078125
- master: float32 [32, 4096, 512], P('rep', 'fsdp'), may hold values from -6 to 6
- moment_one: float32 [32, 4096, 512], P('rep', 'fsdp'), may hold values from -4 to 4
- moment_two: float32 [32, 4096, 512], P('rep', 'fsdp'), may hold values from 0.01 to 1
- push_weight: float32 [32], P('rep'), may hold values from 0.5 to 2
- step_index: int32 [1], replicated, may hold values from 0 to 999
Outputs:
- master_new: float32 [32, 4096, 512], P('rep', 'fsdp')
- moment_one_new: float32 [32, 4096, 512], P('rep', 'fsdp')
- moment_two_new: float32 [32, 4096, 512], P('rep', 'fsdp')
- weight_new: float32 [32], P('rep')
- params_copy: bfloat16 [32, 4096, 512], P('rep', 'fsdp')
All inputs are finite; a program needn't handle non-finite values.
Results may differ from a plain program's by a relative error of at most 0.01.
Values may be sent and summed in bfloat16 or wider, within the bound.
No kernel may reach another device: no remote copies, remote signals or barrier semaphores. Data moves between devices by JAX's collectives and lax.ppermute only.
A program may use at most 128 MiB of HBM per device.

v0:
```python
from functools import partial

import jax
import jax.numpy as jnp
from jax import lax
from jax.sharding import PartitionSpec as P

BETA_ONE = 0.9
BETA_TWO = 0.95
LEARN_RATE = 0.01
DECAY_RATE = 0.1
EPSILON = 1e-08


def from_partner(block, axis, bit):
    count = lax.axis_size(axis)
    route = []
    for low in range(count):
        high = low | 1 << bit
        if high != low and high < count:
            route += [(low, high), (high, low)]
    return lax.ppermute(block, axis, route)


def push_to(bit_number, payload):
    return from_partner(payload, "rep", bit_number)


def on_device(activations, cotangent, master, moment_one, moment_two, push_weight, step_index):
    gradient = lax.psum_scatter(
        lax.dot_general(
            activations, cotangent, (((0,), (0,)), ((), ())), preferred_element_type=jnp.float32
        ).astype(jnp.bfloat16),
        "fsdp",
        scatter_dimension=0,
        tiled=True,
    ).astype(jnp.float32)
    gradient = gradient[None]
    counter = step_index[0]
    steps_done = (counter + 1).astype(jnp.float32)
    first = BETA_ONE * moment_one + (1.0 - BETA_ONE) * gradient
    second = BETA_TWO * moment_two + (1.0 - BETA_TWO) * gradient * gradient
    corr_one = 1.0 - jnp.power(jnp.float32(BETA_ONE), steps_done)
    corr_two = 1.0 - jnp.power(jnp.float32(BETA_TWO), steps_done)
    direction = first / corr_one / (jnp.sqrt(second / corr_two) + EPSILON)
    weights = push_weight[:, None, None]
    halfway = master - LEARN_RATE * (direction + DECAY_RATE * master / weights)
    bit_count = lax.axis_size("rep").bit_length() - 1
    offset = counter % bit_count
    branches = [partial(push_to, bit_number) for bit_number in range(bit_count)]
    other_half, other_first, other_weight = lax.switch(
        offset, branches, (halfway, first, push_weight)
    )
    master_new = 0.5 * (halfway + other_half)
    first_new = 0.5 * (first + other_first)
    weight_new = 0.5 * (push_weight + other_weight)
    params_copy = (master_new / weight_new[:, None, None]).astype(jnp.bfloat16)
    return (master_new, first_new, second, weight_new, params_copy)


def solution(mesh):
    placed = (
        P(("rep", "fsdp"), None),
        P(("rep", "fsdp"), None),
        P("rep", "fsdp", None),
        P("rep", "fsdp", None),
        P("rep", "fsdp", None),
        P("rep"),
        P(),
    )
    return jax.shard_map(
        on_device,
        mesh=mesh,
        in_specs=placed,
        out_specs=(
            P("rep", "fsdp", None),
            P("rep", "fsdp", None),
            P("rep", "fsdp", None),
            P("rep"),
            P("rep", "fsdp", None),
        ),
        check_vma=False,
    )
```

profile of v0, /device:TPU:67, one launch (start us, length us, event | category | flops | bytes accessed | tf_op | source)
XLA Modules:
  0.0 143.0 jit_solution(5145709146137346604)
XLA Ops:
  7.2 0.0 copy-start
  7.2 0.0 reduce-scatter.2.cloned.1.call-start
  7.2 1.1 copy-done
  8.3 7.9 %convolution_convert_fusion = bf16[4096,512]{1,0:T(8,128)(2,1)} fusion(bf16[704,4096]{1,0:T(8,128)(2,1)} %param.12, bf16[704,512]{1,0:T(8,128)(2,1)S(1)} %copy-done), kind=kOutput, calls=%fused_computation | convolution fusion | flops 2954887168 | bytes 10682368 | tf_op jit(solution)/shard_map/dot_general | solution.py:31
  16.1 0.0 reduce-scatter.2.cloned.1.call-update
  17.6 61.7 %reduce-scatter.2.cloned.1.call-done = bf16[512,512]{1,0:T(8,128)(2,1)} async-done(((bf16[4096,512]{1,0:T(8,128)(2,1)}), bf16[512,512]{1,0:T(8,128)(2,1)}) %reduce-scatter.2.cloned.1.call-update) | async-done | bytes 524304 | tf_op jit(solution)/shard_map/reduce_scatter | solution.py:30
  79.3 3.8 %multiply_subtract_fusion = (f32[1,512,512]{2,1,0:T(8,128)S(1)}, f32[1,512,512]{2,1,0:T(8,128)}, f32[1,512,512]{2,1,0:T(8,128)S(1)}) fusion(f32[1,512,512]{2,1,0:T(8,128)} %param.14, f32[]{:T(128)} %bitcast.17, f32[]{:T(128)} %bitcast.3, f32[]{:T(128)} %bitcast.1, bf16[512,512]{1,0:T(8,128)(2,1)} %reduce-scatter.2.cloned.1.call-done, ...), kind=kLoop, calls=%fused_computation.10 | loop fusion | flops 4456448 | bytes 6815756 | tf_op jit(solution)/shard_map/sub | solution.py:47
  83.1 48.0 %conditional.1 = (f32[1,512,512]{2,1,0:T(8,128)}, f32[1,512,512]{2,1,0:T(8,128)}, f32[1]{0:T(128)}) conditional(s32[]{:T(128)} %clamp.3, (f32[1,512,512]{2,1,0:T(8,128)S(1)}, f32[1,512,512]{2,1,0:T(8,128)S(1)}, f32[1]{0:T(128)}) %tuple.28, (f32[1,512,512]{2,1,0:T(8,128)S(1)}, f32[1,512,512]{2,1,0:T(8,128)S(1)}, ...), branch_computations={%region_1.2_spmd, %region_2.3_spmd, %region_3.4_spmd, %region_4.5_... | conditional | bytes 8388768 | solution.py:51
  83.1 1.2 collective-permute-start.9
  84.3 1.8 %collective-permute-start.10 = (f32[1,512,512]{2,1,0:T(8,128)S(1)}, f32[1,512,512]{2,1,0:T(8,128)}, u32[]{:S(2)}, u32[]{:S(2)}) collective-permute-start(f32[1,512,512]{2,1,0:T(8,128)S(1)} %get-tuple-element.40), channel_id=1, source_target_pairs={{0,64},{64,0},{8,72},{72,8},{16,80},{80,16},{24,88},{88,24},{32,96... | collective-permute-start | bytes 3145736 | tf_op jit(solution)/shard_map/cond/branch_3_fun/ppermute | solution.py:22
  86.1 1.2 collective-permute-start.11
  87.3 43.9 %collective-permute-done.11 = f32[1]{0:T(128)} collective-permute-done((f32[1]{0:T(128)}, f32[1]{0:T(128)}, u32[]{:S(2)}, u32[]{:S(2)}) %collective-permute-start.11) | collective-permute-done | bytes 36 | tf_op jit(solution)/shard_map/cond/branch_3_fun/ppermute | solution.py:22
  131.2 0.0 collective-permute-done.9
  131.2 0.0 collective-permute-done.10
  131.7 3.3 %divide_convert_fusion = (bf16[1,512,512]{2,1,0:T(8,128)(2,1)}, f32[1,512,512]{2,1,0:T(8,128)}, f32[1,512,512]{2,1,0:T(8,128)}) fusion(f32[]{:T(128)} %bitcast.6, f32[1,512,512]{2,1,0:T(8,128)S(1)} %get-tuple-element.58, f32[1,512,512]{2,1,0:T(8,128)} %get-tuple-element.53, f32[1,512,512]{2,1,0:T(8,128)S(1)} %get-tuple-element.60, ...), kind=kLoop, calls=%fused_computation.7 | loop fusion | flops 1572864 | bytes 6815748 | tf_op jit(solution)/shard_map/convert_element_type | solution.py:57
Async XLA Ops:
  7.2 1.1 copy-start
  7.2 72.1 %reduce-scatter.2.cloned.1.call-start = ((), (), s32[]{:S(2)}) async-start(), calls=%async_computation.1 | async-start | bytes 4718592 | tf_op jit(solution)/shard_map/reduce_scatter | solution.py:30
  83.1 48.0 %collective-permute-start.9 = (f32[1,512,512]{2,1,0:T(8,128)S(1)}, f32[1,512,512]{2,1,0:T(8,128)}, u32[]{:S(2)}, u32[]{:S(2)}) collective-permute-start(f32[1,512,512]{2,1,0:T(8,128)S(1)} %get-tuple-element.39), channel_id=1, source_target_pairs={{0,64},{64,0},{8,72},{72,8},{16,80},{80,16},{24,88},{88,24},{32,96... | collective-permute-start | bytes 3145736 | tf_op jit(solution)/shard_map/cond/branch_3_fun/ppermute | solution.py:22
  84.3 46.9 %collective-permute-start.10 = (f32[1,512,512]{2,1,0:T(8,128)S(1)}, f32[1,512,512]{2,1,0:T(8,128)}, u32[]{:S(2)}, u32[]{:S(2)}) collective-permute-start(f32[1,512,512]{2,1,0:T(8,128)S(1)} %get-tuple-element.40), channel_id=1, source_target_pairs={{0,64},{64,0},{8,72},{72,8},{16,80},{80,16},{24,88},{88,24},{32,96... | collective-permute-start | bytes 3145736 | tf_op jit(solution)/shard_map/cond/branch_3_fun/ppermute | solution.py:22
  86.1 45.1 %collective-permute-start.11 = (f32[1]{0:T(128)}, f32[1]{0:T(128)}, u32[]{:S(2)}, u32[]{:S(2)}) collective-permute-start(f32[1]{0:T(128)} %get-tuple-element.41), channel_id=1, source_target_pairs={{0,64},{64,0},{8,72},{72,8},{16,80},{80,16},{24,88},{88,24},{32,96... | collective-permute-start | bytes 20 | tf_op jit(solution)/shard_map/cond/branch_3_fun/ppermute | solution.py:22
Sparse Core Ops, SparseCore 0:
  16.3 62.9 reduce-scatter.1
where the time goes:
time: 142 us; the launch traced here: 143 us
  waiting for transfers between devices  106 us (75%)
  between operations  17.1 us (12%)
  matrix products  7.86 us (6%)
  other arithmetic  7.12 us (5%)
  starting transfers between devices  4.18 us (3%)
    reduce_scatter x1, waiting for transfers between devices, on_device(): lax.psum_scatter(lax.dot_general(activations, cotangent, (((0,), (0,)), (...  61.7 us
    ppermute x3, waiting for transfers between devices, from_partner(): return lax.ppermute(block, axis, route)  43.9 us
    dot_general x1, matrix products, on_device(): lax.dot_general(activations, cotangent, (((0,), (0,)), ((), ())), preferr...  7.86 us
    ppermute x3, starting transfers between devices, from_partner(): return lax.ppermute(block, axis, route)  4.14 us
    sub x1, other arithmetic, on_device(): halfway = master - LEARN_RATE * (direction + DECAY_RATE * master / weights)  3.83 us
    convert_element_type x1, other arithmetic, on_device(): params_copy = (master_new / weight_new[:, None, None]).astype(jnp.bfloat16)  3.29 us
  transfers between devices with their start and end apart: 4, of which 2 were waited for; matrix products, arithmetic and copies ran while one was open for 0% of the time, Pallas kernels for 0%

commit v1 on v0

v1 whole, which is shorter than its diff:
```python
import math
from functools import partial

import jax
import jax.numpy as jnp
from jax import lax
from jax.experimental import pallas as pl
from jax.experimental.pallas import tpu as pltpu
from jax.sharding import PartitionSpec as P

BETA_ONE = 0.9
BETA_TWO = 0.95
LEARN_RATE = 0.01
DECAY_RATE = 0.1
EPSILON = 1e-08

F32 = jnp.float32
BF16 = jnp.bfloat16
HBM = pl.BlockSpec(memory_space=pltpu.HBM)
SMEM = pl.BlockSpec(memory_space=pltpu.SMEM)
VMEM = pl.BlockSpec(memory_space=pltpu.VMEM)
PARAMS = pltpu.CompilerParams(vmem_limit_bytes=16 * 1024 * 1024)
SMALL = pl.CostEstimate(flops=0, bytes_accessed=0, transcendentals=0)
CHUNKS = ((0, 256), (256, 256))
PARTS = 4


def shape(dtype, *sizes):
    return pltpu.VMEM(sizes, dtype)


def in_hbm(array):
    return pltpu.with_memory_space_constraint(array, pltpu.HBM)


def product(x, g):
    return lax.dot_general(x, g, (((0,), (0,)), ((), ())), preferred_element_type=F32)


class Blocks:
    def __init__(self, x, g, x_held, g_held, x_sems, g_sems, columns):
        tokens, width = x_held.shape[1:]
        part = tokens // PARTS
        rows = [pl.ds(i * part, part) for i in range(PARTS)]
        self.g_copies = [pltpu.make_async_copy(g.at[at], g_held.at[at], g_sems.at[i]) for i, at in enumerate(rows)]
        self.x_copies = [
            [
                pltpu.make_async_copy(
                    x.at[at, pl.ds(pl.multiple_of(low, width), width)], x_held.at[k, at], x_sems.at[PARTS * k + i]
                )
                for i, at in enumerate(rows)
            ]
            for k, low in enumerate(columns)
        ]
        self.x_held, self.g_held = x_held, g_held
        for copy in self.g_copies:
            copy.start()
        for copies in self.x_copies[:2]:
            for copy in copies:
                copy.start()

    def product(self, k):
        if k == 0:
            for copy in self.g_copies:
                copy.wait()
        for copy in self.x_copies[k]:
            copy.wait()
        for copies in self.x_copies[k + 2 : k + 3]:
            for copy in copies:
                copy.start()
        return product(self.x_held[k], self.g_held[...])

    @staticmethod
    def scratch(blocks, tokens, width, columns):
        return [
            pltpu.VMEM((blocks, tokens, width), BF16),
            pltpu.VMEM((tokens, columns), BF16),
            pltpu.SemaphoreType.DMA((PARTS * blocks,)),
            pltpu.SemaphoreType.DMA((PARTS,)),
        ]


def first_column(me, ahead, other, width, groups):
    group, core = lax.shift_right_logical(me[0], 1), lax.bitwise_and(me[0], 1)
    return (2 * lax.rem(group + ahead, groups) + (1 - core if other else core)) * width


def others_kernel(aheads, me, x, g, out, *scratch):
    width = out.shape[0] // len(aheads)
    groups = x.shape[1] // (2 * width)
    blocks = Blocks(x, g, *scratch, [first_column(me, d % groups, True, width, groups) for d in aheads])
    for k in range(len(aheads)):
        out[pl.ds(k * width, width)] = blocks.product(k).astype(BF16)


def other_blocks(aheads, me, x, g, width):
    tokens, columns = g.shape
    return pl.pallas_call(
        partial(others_kernel, aheads),
        in_specs=[SMEM, HBM, HBM],
        out_specs=VMEM,
        out_shape=shape(BF16, len(aheads) * width, columns),
        scratch_shapes=Blocks.scratch(len(aheads), tokens, width, columns),
        compiler_params=PARAMS,
        cost_estimate=SMALL,
        name="other_blocks",
    )(me, x, g)


def far_kernel(me, x, g, got, *rest):
    up, down, *scratch = rest
    width = got.shape[0]
    groups = x.shape[1] // (2 * width)
    total = Blocks(x, g, *scratch, [first_column(me, 2, False, width, groups)]).product(0) + got[...].astype(F32)
    to = 0
    for low, rows in CHUNKS:
        half = rows // 2
        up[to : to + half] = total[low : low + half].astype(BF16)
        down[to : to + half] = total[low + half : low + rows].astype(BF16)
        to += half


def far_block(me, x, g, got):
    outs = [shape(BF16, got.shape[0] // 2, g.shape[1])] * 2
    return pl.pallas_call(
        far_kernel,
        in_specs=[SMEM, HBM, HBM, VMEM],
        out_specs=[VMEM] * len(outs),
        out_shape=outs,
        scratch_shapes=Blocks.scratch(1, g.shape[0], *got.shape),
        compiler_params=PARAMS,
        cost_estimate=SMALL,
        name="far_block",
    )(me, x, g, got)


def near_kernel(me, x, g, got, *rest):
    b_up, b_down, c_up_1, c_down_1, c_up_2, c_down_2, own_1, own_2 = rest[:8]
    width = got.shape[0] // 3
    groups = x.shape[1] // (2 * width)
    blocks = Blocks(x, g, *rest[8:], [first_column(me, d, False, width, groups) for d in (1, groups - 1, 0)])
    (low_1, rows_1), (low_2, rows_2) = CHUNKS
    half_1, half_2 = rows_1 // 2, rows_2 // 2

    def total(k):
        return blocks.product(k) + got[pl.ds(k * width, width)].astype(F32)

    above = total(0)
    c_up_1[...] = above[low_1 : low_1 + half_1]
    b_up[:half_1] = above[low_1 + half_1 : low_1 + rows_1].astype(BF16)
    c_up_2[...] = above[low_2 : low_2 + half_2]
    b_up[half_1:] = above[low_2 + half_2 : low_2 + rows_2].astype(BF16)
    below = total(1)
    b_down[:half_1] = below[low_1 : low_1 + half_1].astype(BF16)
    c_down_1[...] = below[low_1 + half_1 : low_1 + rows_1]
    b_down[half_1:] = below[low_2 : low_2 + half_2].astype(BF16)
    c_down_2[...] = below[low_2 + half_2 : low_2 + rows_2]
    own = total(2)
    own_1[...] = own[low_1 : low_1 + rows_1]
    own_2[...] = own[low_2 : low_2 + rows_2]


def near_blocks(me, x, g, got):
    columns = g.shape[1]
    (_, rows_1), (_, rows_2) = CHUNKS
    half_1, half_2 = rows_1 // 2, rows_2 // 2
    outs = [shape(BF16, half_1 + half_2, columns)] * 2
    outs += [shape(F32, half_1, columns)] * 2 + [shape(F32, half_2, columns)] * 2
    outs += [shape(F32, rows_1, columns), jax.ShapeDtypeStruct((rows_2, columns), F32)]
    return pl.pallas_call(
        near_kernel,
        in_specs=[SMEM, HBM, HBM, VMEM],
        out_specs=[VMEM] * len(outs),
        out_shape=outs,
        scratch_shapes=Blocks.scratch(3, g.shape[0], got.shape[0] // 3, columns),
        compiler_params=PARAMS,
        cost_estimate=SMALL,
        name="near_blocks",
    )(me, x, g, got)


def add_kernel(low, up, got_up, down, got_down, *rest):
    at = pl.ds(low, up.shape[0])
    for mine, got, out in ((up, got_up, rest[-2]), (down, got_down, rest[-1])):
        out[...] = (mine[...] + got[at].astype(F32)).astype(BF16)


def add_far(low, up, got_up, down, got_down, earlier=()):
    return pl.pallas_call(
        partial(add_kernel, low),
        in_specs=[VMEM] * 4 + [HBM] * len(earlier),
        out_specs=[VMEM] * 2,
        out_shape=[shape(BF16, *up.shape)] * 2,
        compiler_params=PARAMS,
        cost_estimate=SMALL,
        name="add_far",
    )(up, got_up, down, got_down, *earlier)


def fetch_kernel(places, *refs):
    count = len(places)
    copies = []
    for i, (start, rows) in enumerate(places):
        source, held, sems = refs[i], refs[count + i], refs[2 * count]
        part = rows // 2
        for k in range(2):
            copies.append(
                pltpu.make_async_copy(
                    source.at[pl.ds(start + k * part, part)], held.at[pl.ds(k * part, part)], sems.at[2 * i + k]
                )
            )
            copies[-1].start()
    for copy in copies:
        copy.wait()


def fetch(places, *arrays):
    return pl.pallas_call(
        partial(fetch_kernel, places),
        in_specs=[HBM] * len(arrays),
        out_specs=[VMEM] * len(arrays),
        out_shape=[shape(a.dtype, rows, a.shape[1]) for a, (_, rows) in zip(arrays, places)],
        scratch_shapes=[pltpu.SemaphoreType.DMA((2 * len(arrays),))],
        compiler_params=PARAMS,
        cost_estimate=SMALL,
        name="fetch",
    )(*arrays)


def step_kernel(start, low_b, step, push_weight, own, c_up, c_down, b_up, b_down, master, one, two, *refs):
    second_out, halfway_out, first_out, send, second_made, halfway_made, first_made, sems = refs[-8:]
    copies = []
    rows, columns = own.shape
    half = rows // 2
    row = (1, columns)
    number = jnp.full(row, step[0] + 1, jnp.int32).astype(F32)
    scale_one = 1.0 / (1.0 - jnp.exp(number * math.log(BETA_ONE)))
    scale_two = 1.0 / (1.0 - jnp.exp(number * math.log(BETA_TWO)))
    decay = DECAY_RATE / jnp.full(row, push_weight[0], F32)
    for low, c, b in ((0, c_up, b_down), (half, c_down, b_up)):
        at = pl.ds(low, half)
        gradient = own[at] + (c[...].astype(F32) + b[pl.ds(low_b, half)].astype(F32))
        first = BETA_ONE * one[at] + (1.0 - BETA_ONE) * gradient
        second = BETA_TWO * two[at] + (1.0 - BETA_TWO) * gradient * gradient
        direction = first * scale_one / (jnp.sqrt(second * scale_two) + EPSILON)
        weights = master[at]
        halfway = weights - LEARN_RATE * (direction + weights * decay)
        second_made[at] = second
        halfway_made[at] = halfway
        first_made[at] = first
        send[at] = halfway.astype(BF16)
        send[pl.ds(rows + low, half)] = first.astype(BF16)
        for made, out, place in (
            (second_made, second_out, start + low),
            (halfway_made, halfway_out, low),
            (first_made, first_out, low),
        ):
            copies.append(pltpu.make_async_copy(made.at[at], out.at[pl.ds(place, half)], sems.at[len(copies)]))
            copies[-1].start()
    for copy in copies:
        copy.wait()


def step_chunk(start, height, low_b, ins, before=(), earlier=()):
    rows, columns = ins[2].shape
    return pl.pallas_call(
        partial(step_kernel, start, low_b),
        in_specs=[SMEM] * 2 + [VMEM] * (len(ins) - 2) + [HBM] * (len(before) + len(earlier)),
        out_specs=[HBM] * 3 + [VMEM],
        out_shape=[pltpu.HBM((height, columns), F32)]
        + [pltpu.HBM((rows, columns), F32)] * 2
        + [shape(BF16, 2 * rows, columns)],
        scratch_shapes=[pltpu.VMEM((rows, columns), F32)] * 3 + [pltpu.SemaphoreType.DMA((6,))],
        input_output_aliases={len(ins): 0} if before else {},
        compiler_params=PARAMS,
        cost_estimate=SMALL,
        name="step_chunk",
    )(*ins, *before, *earlier)


def mix_kernel(start, rows, push_weight, other_weight, halfway, first, got, *rest):
    master_out, first_out, copy_out, master_new, first_new, copy, in_sems, out_sems = rest[-8:]
    pieces = 2
    part = rows // pieces
    row = (1, got.shape[1])
    at = [pl.ds(k * part, part) for k in range(pieces)]
    to = [pl.ds(start + k * part, part) for k in range(pieces)]
    loads = [
        [
            pltpu.make_async_copy(source.at[at[k]], held.at[at[k]], in_sems.at[2 * k + i])
            for i, (source, held) in enumerate(((halfway, master_new), (first, first_new)))
        ]
        for k in range(pieces)
    ]
    for pair in loads:
        for load in pair:
            load.start()
    copies = []
    scale = 1.0 / (0.5 * (jnp.full(row, push_weight[0], F32) + jnp.full(row, other_weight[0], F32)))
    for k in range(pieces):
        for load in loads[k]:
            load.wait()
        mixed = 0.5 * (master_new[at[k]] + got[at[k]].astype(F32))
        master_new[at[k]] = mixed
        copy[at[k]] = (mixed * scale).astype(BF16)
        first_new[at[k]] = 0.5 * (first_new[at[k]] + got[pl.ds(rows + k * part, part)].astype(F32))
        for i, (made, out) in enumerate(((master_new, master_out), (first_new, first_out), (copy, copy_out))):
            send = pltpu.make_async_copy(made.at[at[k]], out.at[to[k]], out_sems.at[3 * k + i])
            send.start()
            copies.append(send)
    for send in copies:
        send.wait()


def mix_chunk(start, rows, height, push_weight, other_weight, halfway, first, got, before=()):
    columns = halfway.shape[1]
    ins = (push_weight, other_weight, in_hbm(halfway), in_hbm(first), got)
    return pl.pallas_call(
        partial(mix_kernel, start, rows),
        in_specs=[SMEM] * 2 + [HBM] * 2 + [VMEM] + [HBM] * len(before),
        out_specs=[HBM] * 3,
        out_shape=[pltpu.HBM((height, columns), F32)] * 2 + [pltpu.HBM((height, columns), BF16)],
        scratch_shapes=[
            pltpu.VMEM((rows, columns), F32),
            pltpu.VMEM((rows, columns), F32),
            pltpu.VMEM((rows, columns), BF16),
            pltpu.SemaphoreType.DMA((4,)),
            pltpu.SemaphoreType.DMA((6,)),
        ],
        input_output_aliases={len(ins) + i: i for i in range(len(before))},
        compiler_params=PARAMS,
        cost_estimate=SMALL,
        name="mix_chunk",
    )(*ins, *before)


def up_z(block):
    count = lax.axis_size("fsdp")
    return lax.ppermute(block, "fsdp", [(i, (i + 2) % count) for i in range(count)])


def down_z(block):
    count = lax.axis_size("fsdp")
    return lax.ppermute(block, "fsdp", [(i, (i - 2) % count) for i in range(count)])


def other_core(block):
    return lax.ppermute(block, "fsdp", [(i, i ^ 1) for i in range(lax.axis_size("fsdp"))])


def from_partner(block, bit):
    return lax.ppermute(block, "rep", [(i, i ^ (1 << bit)) for i in range(lax.axis_size("rep"))])


def after(value, *earlier):
    return lax.optimization_barrier((value, *earlier))[0]


def first_exchange(bit, send, push_weight):
    return from_partner(send, bit), from_partner(push_weight, bit)


def second_exchange(height, bit, send, *mix):
    return (from_partner(send, bit), *mix_chunk(*CHUNKS[0], height, *mix))


def on_device(activations, cotangent, master, moment_one, moment_two, push_weight, step_index):
    x, g, state = in_hbm(activations), in_hbm(cotangent), [in_hbm(v[0]) for v in (master, moment_one, moment_two)]
    height = master.shape[1]
    bits = lax.axis_size("rep").bit_length() - 1

    def with_partner(exchange, *values):
        return lax.switch(lax.rem(step_index[0], bits), [partial(exchange, bit) for bit in range(bits)], *values)

    me = jnp.full((1,), lax.axis_index("fsdp"), jnp.int32)
    (low_1, rows_1), (low_2, rows_2) = CHUNKS
    half_1, half_2 = rows_1 // 2, rows_2 // 2
    out_far = other_blocks((2,), me, x, g, height)
    out_near = other_blocks((1, -1, 0), after(me, out_far), x, g, height)
    got_far = other_core(out_far)
    got_near = other_core(after(out_near, got_far))
    a_up, a_down = far_block(after(me, out_near), x, g, got_far)
    got_a_up, got_a_down = up_z(a_up), down_z(a_down)
    state_1 = fetch([(low_1, rows_1)] * 3, *(after(v, a_up) for v in state))
    b_up, b_down, c_up_1, c_down_1, c_up_2, c_down_2, own_1, own_2 = near_blocks(
        me, x, g, after(got_near, state_1[0])
    )
    got_b = up_z(b_up), down_z(b_down)
    c_up_1, c_down_1 = add_far(0, c_up_1, got_a_up, c_down_1, got_a_down)
    got_c = up_z(c_up_1), down_z(c_down_1)
    rest = add_far(half_1, c_up_2, got_a_up, c_down_2, got_a_down, got_b)
    got_rest = up_z(rest[0]), down_z(rest[1])
    scalars = step_index, push_weight
    second, *made_1 = step_chunk(low_1, height, 0, (*scalars, own_1, *got_c, *got_b, *state_1), (), rest)
    got_1, other_weight = with_partner(first_exchange, made_1[2], push_weight)
    weights = push_weight, other_weight
    places_2 = [(low_2, rows_2)] * 3 + [(0, rows_2)]
    *state_2, own_2 = fetch(places_2, *(after(v, got_1) for v in (*state, own_2)))
    second, *made_2 = step_chunk(
        low_2, height, half_1, (*scalars, own_2, *got_rest, *got_b, *state_2), (second,)
    )
    got_2, *mixed = with_partner(partial(second_exchange, height), made_2[2], *weights, *made_1[:2], got_1)
    mixed, first, copy = mix_chunk(*CHUNKS[1], height, *weights, *made_2[:2], got_2, mixed)
    weight_new = 0.5 * (push_weight + other_weight)
    return (mixed[None], first[None], second[None], weight_new, copy[None])


def solution(mesh):
    placed = (
        P(("rep", "fsdp"), None),
        P(("rep", "fsdp"), None),
        P("rep", "fsdp", None),
        P("rep", "fsdp", None),
        P("rep", "fsdp", None),
        P("rep"),
        P(),
    )
    return jax.shard_map(
        on_device,
        mesh=mesh,
        in_specs=placed,
        out_specs=(
            P("rep", "fsdp", None),
            P("rep", "fsdp", None),
            P("rep", "fsdp", None),
            P("rep"),
            P("rep", "fsdp", None),
        ),
        check_vma=False,
    )
```

time: 142 us -> 86.7 us (0.61)
  the two profiles are of different devices: /device:TPU:67 before, /device:TPU:6 now
where the time goes in v1:
time: 86.7 us; the launch traced here: 85.7 us
  waiting for transfers between devices  34.2 us (39%)
  Pallas kernels  25.3 us (29%)
  starting transfers between devices  22 us (25%)
  between operations  3.85 us (4%)
    ppermute x3, waiting for transfers between devices, from_partner(): lax.ppermute(block, 'rep', [(i, i ^ 1 << bit) for i in range(lax.axis_siz...  20.2 us
    ppermute x4, starting transfers between devices, down_z(): lax.ppermute(block, 'fsdp', [(i, (i - 2) % count) for i in range(count)])  9.66 us
    ppermute x4, starting transfers between devices, up_z(): lax.ppermute(block, 'fsdp', [(i, (i + 2) % count) for i in range(count)])  9.46 us
    pallas_call x2, Pallas kernels, mix_chunk(): pl.pallas_call(partial(mix_kernel, start, rows), in_specs=[SMEM] * 2 + [H...  8.37 us
    ppermute x4, waiting for transfers between devices, up_z(): lax.ppermute(block, 'fsdp', [(i, (i + 2) % count) for i in range(count)])  7.44 us
    ppermute x4, waiting for transfers between devices, down_z(): lax.ppermute(block, 'fsdp', [(i, (i - 2) % count) for i in range(count)])  6.54 us
    pallas_call x2, Pallas kernels, other_blocks(): pl.pallas_call(partial(others_kernel, aheads), in_specs=[SMEM, HBM, HBM],...  5.65 us
    pallas_call x1, Pallas kernels, near_blocks(): pl.pallas_call(near_kernel, in_specs=[SMEM, HBM, HBM, VMEM], out_specs=[V...  3.58 us
  transfers between devices with their start and end apart: 13, of which 4 were waited for; matrix products, arithmetic and copies ran while one was open for 0% of the time, Pallas kernels for 21%

profile of v1, /device:TPU:6, one launch (start us, length us, event | category | flops | bytes accessed | tf_op | source)
XLA Modules:
  0.0 85.7 jit_solution(5096889027500954997)
XLA Ops:
  0.6 2.1 %other_blocks.2 = bf16[512,512]{1,0:T(8,128)(2,1)S(1)} custom-call(s32[1]{0:T(128)} %bitcast.1.me, bf16[704,4096]{1,0:T(8,128)(2,1)} %x.7, bf16[704,512]{1,0:T(8,128)(2,1)} %g.7), custom_call_target="tpu_custom_call" | custom-call | tf_op jit(solution)/shard_map/other_blocks/pallas_call | solution.py:98
  2.7 0.1 collective-permute-start.15
  2.8 3.6 %other_blocks.3 = bf16[1536,512]{1,0:T(8,128)(2,1)S(1)} custom-call(s32[1]{0:T(128)} %bitcast.1.me, bf16[704,4096]{1,0:T(8,128)(2,1)} %x.7, bf16[704,512]{1,0:T(8,128)(2,1)} %g.7), custom_call_target="tpu_custom_call" | custom-call | tf_op jit(solution)/shard_map/other_blocks/pallas_call | solution.py:98
  6.4 0.0 collective-permute-done.15.got
  6.4 0.6 collective-permute-start.16
  7.0 2.1 %far_block.1 = (bf16[256,512]{1,0:T(8,128)(2,1)S(1)}, bf16[256,512]{1,0:T(8,128)(2,1)S(1)}) custom-call(s32[1]{0:T(128)} %bitcast.1.me, bf16[704,4096]{1,0:T(8,128)(2,1)} %x.7, bf16[704,512]{1,0:T(8,128)(2,1)} %g.7, bf16[512,512]{1,0:T(8,128)(2,1)S(1)} %collective-permute-done.15.got), custom_call_target="tpu_custom_call" | custom-call | tf_op jit(solution)/shard_map/far_block/pallas_call | solution.py:125
  9.1 3.4 %collective-permute-start.17 = (bf16[256,512]{1,0:T(8,128)(2,1)S(1)}, bf16[256,512]{1,0:T(8,128)(2,1)S(1)}, u32[]{:S(2)}, u32[]{:S(2)}) collective-permute-start(bf16[256,512]{1,0:T(8,128)(2,1)S(1)} %get-tuple-element.192), channel_id=1, source_target_pairs={{0,2},{1,3},{2,4},{3,5},{4,6},{5,7},{6,0},{7,1},{8,10},{9,11},{10,... | collective-permute-start | bytes 786440 | tf_op jit(solution)/shard_map/ppermute | solution.py:339
  12.4 3.1 %collective-permute-start.18 = (bf16[256,512]{1,0:T(8,128)(2,1)S(1)}, bf16[256,512]{1,0:T(8,128)(2,1)S(1)}, u32[]{:S(2)}, u32[]{:S(2)}) collective-permute-start(bf16[256,512]{1,0:T(8,128)(2,1)S(1)} %get-tuple-element.201), channel_id=1, source_target_pairs={{0,6},{1,7},{2,0},{3,1},{4,2},{5,3},{6,4},{7,5},{8,14},{9,15},{10,... | collective-permute-start | bytes 786440 | tf_op jit(solution)/shard_map/ppermute | solution.py:344
  15.5 1.4 %fetch.2 = (f32[256,512]{1,0:T(8,128)S(1)}, f32[256,512]{1,0:T(8,128)S(1)}, f32[256,512]{1,0:T(8,128)S(1)}) custom-call(f32[512,512]{1,0:T(8,128)} %bitcast.9, f32[512,512]{1,0:T(8,128)} %bitcast.11, f32[512,512]{1,0:T(8,128)} %bitcast.13), custom_call_target="tpu_custom_call" | custom-call | tf_op jit(solution)/shard_map/fetch/pallas_call | solution.py:218
  16.9 0.0 collective-permute-done.16.got
  17.0 3.6 %near_blocks.1 = (bf16[256,512]{1,0:T(8,128)(2,1)S(1)}, bf16[256,512]{1,0:T(8,128)(2,1)S(1)}, f32[128,512]{1,0:T(8,128)S(1)}, f32[128,512]{1,0:T(8,128)S(1)}, f3...) custom-call(s32[1]{0:T(128)} %bitcast.1.me, ...), custom_call_target="tpu_custom_call" | custom-call | tf_op jit(solution)/shard_map/near_blocks/pallas_call | solution.py:170
  20.5 1.4 %collective-permute-start.21 = (bf16[256,512]{1,0:T(8,128)(2,1)S(1)}, bf16[256,512]{1,0:T(8,128)(2,1)S(1)}, u32[]{:S(2)}, u32[]{:S(2)}) collective-permute-start(bf16[256,512]{1,0:T(8,128)(2,1)S(1)} %get-tuple-element.204), channel_id=1, source_target_pairs={{0,2},{1,3},{2,4},{3,5},{4,6},{5,7},{6,0},{7,1},{8,10},{9,11},{10,... | collective-permute-start | bytes 786440 | tf_op jit(solution)/shard_map/ppermute | solution.py:339
  22.0 2.8 %collective-permute-start.22 = (bf16[256,512]{1,0:T(8,128)(2,1)S(1)}, bf16[256,512]{1,0:T(8,128)(2,1)S(1)}, u32[]{:S(2)}, u32[]{:S(2)}) collective-permute-start(bf16[256,512]{1,0:T(8,128)(2,1)S(1)} %get-tuple-element.205), channel_id=1, source_target_pairs={{0,6},{1,7},{2,0},{3,1},{4,2},{5,3},{6,4},{7,5},{8,14},{9,15},{10,... | collective-permute-start | bytes 786440 | tf_op jit(solution)/shard_map/ppermute | solution.py:344
  24.8 0.0 collective-permute-done.17.got_up
  24.8 6.5 %collective-permute-done.18.got_down = bf16[256,512]{1,0:T(8,128)(2,1)S(1)} collective-permute-done((bf16[256,512]{1,0:T(8,128)(2,1)S(1)}, bf16[256,512]{1,0:T(8,128)(2,1)S(1)}, u32[]{:S(2)}, u32[]{:S(2)}) %collective-permute-start.18) | collective-permute-done | bytes 262176 | tf_op jit(solution)/shard_map/ppermute | solution.py:344
  31.3 4.0 %collective-permute-start.19 = (bf16[128,512]{1,0:T(8,128)(2,1)S(1)}, bf16[128,512]{1,0:T(8,128)(2,1)S(1)}, u32[]{:S(2)}, u32[]{:S(2)}) collective-permute-start(bf16[128,512]{1,0:T(8,128)(2,1)S(1)} %get-tuple-element.202), channel_id=1, source_target_pairs={{0,2},{1,3},{2,4},{3,5},{4,6},{5,7},{6,0},{7,1},{8,10},{9,11},{10,... | collective-permute-start | bytes 393224 | tf_op jit(solution)/shard_map/ppermute | solution.py:339
  35.4 0.2 collective-permute-start.20
  35.6 7.4 %collective-permute-done.21.rest_0_.b_up = bf16[256,512]{1,0:T(8,128)(2,1)S(1)} collective-permute-done((bf16[256,512]{1,0:T(8,128)(2,1)S(1)}, bf16[256,512]{1,0:T(8,128)(2,1)S(1)}, u32[]{:S(2)}, u32[]{:S(2)}) %collective-permute-start.21) | collective-permute-done | bytes 262176 | tf_op jit(solution)/shard_map/ppermute | solution.py:339
  43.0 0.0 collective-permute-done.22.rest_1_.b_down
  43.0 0.1 add_far.3
  43.0 0.6 collective-permute-start.23
  43.7 3.6 %collective-permute-start.24 = (bf16[128,512]{1,0:T(8,128)(2,1)S(1)}, bf16[128,512]{1,0:T(8,128)(2,1)S(1)}, u32[]{:S(2)}, u32[]{:S(2)}) collective-permute-start(bf16[128,512]{1,0:T(8,128)(2,1)S(1)} %get-tuple-element.211.refs_1_), channel_id=1, source_target_pairs={{0,6},{1,7},{2,0},{3,1},{4,2},{5,3},{6,4},{7,5},{8,14},{9,15},{10,... | collective-permute-start | bytes 393224 | tf_op jit(solution)/shard_map/ppermute | solution.py:344
  48.6 0.0 collective-permute-done.19.c_up
  48.6 0.0 collective-permute-done.20.c_down
  48.6 1.4 %step_chunk.2 = (f32[512,512]{1,0:T(8,128)}, f32[256,512]{1,0:T(8,128)}, f32[256,512]{1,0:T(8,128)}, bf16[512,512]{1,0:T(8,128)(2,1)S(1)}) custom-call(s32[1]{0:T(128)S(6)} %copy.51.step, f32[1]{0:T(128)S(6)} %copy.50.push_weight, f32[256,512]{1,0:T(8,128)S(1)} %get-tuple-element.198.own, bf16[128,512]{1,0:T(8,128)(2,1)S(1)} %collective-permute-done.19.c_up, ...), custom_call_target="tpu_custom_call" | custom-call | tf_op jit(solution)/shard_map/step_chunk/pallas_call | solution.py:266
  50.0 14.2 %conditional.2 = (bf16[512,512]{1,0:T(8,128)(2,1)}, f32[1]{0:T(128)}) conditional(s32[]{:T(128)} %bitcast, (bf16[512,512]{1,0:T(8,128)(2,1)S(1)}, f32[1]{0:T(128)}) %tuple.66, (bf16[512,512]{1,0:T(8,128)(2,1)S(1)}, f32[1]{0:T(128)}) %tuple.66, (bf16[512,512]{1,0:T(8,128)(2,1)S(1)}, f32[1]{0:T(128)}) %tuple.66, ...), branch_computations={%region_0.0_spmd, %region_1.0_spmd, %region_2.0_spmd, %region_3.0_... | conditional | bytes 2097264 | solution.py:373
  50.2 0.8 collective-permute-start.8
  50.9 1.4 %collective-permute-start.9 = (f32[1]{0:T(128)}, f32[1]{0:T(128)}, u32[]{:S(2)}, u32[]{:S(2)}) collective-permute-start(f32[1]{0:T(128)} %get-tuple-element.89), channel_id=1, source_target_pairs={{0,128},{8,136},{16,144},{24,152},{32,160},{40,168},{48,176},{56,1... | collective-permute-start | bytes 20 | tf_op jit(solution)/shard_map/cond/branch_4_fun/ppermute | solution.py:352
  52.3 11.9 %collective-permute-done.9 = f32[1]{0:T(128)} collective-permute-done((f32[1]{0:T(128)}, f32[1]{0:T(128)}, u32[]{:S(2)}, u32[]{:S(2)}) %collective-permute-start.9) | collective-permute-done | bytes 36 | tf_op jit(solution)/shard_map/cond/branch_4_fun/ppermute | solution.py:352
  64.2 0.0 collective-permute-done.8
  64.9 1.4 %fetch.3 = (f32[256,512]{1,0:T(8,128)S(1)}, f32[256,512]{1,0:T(8,128)S(1)}, f32[256,512]{1,0:T(8,128)S(1)}, f32[256,512]{1,0:T(8,128)S(1)}) custom-call(f32[512,512]{1,0:T(8,128)} %bitcast.10, f32[512,512]{1,0:T(8,128)} %bitcast.12, f32[512,512]{1,0:T(8,128)} %bitcast.14, f32[256,512]{1,0:T(8,128)S(1)} %get-tuple-element.219.refs_3_), custom_call_target="tpu_custom_call" | custom-call | tf_op jit(solution)/shard_map/fetch/pallas_call | solution.py:218
  66.3 0.0 collective-permute-done.23.c_up
  66.3 0.0 collective-permute-done.24.c_down
  66.3 1.4 %step_chunk.3 = (f32[512,512]{1,0:T(8,128)}, f32[256,512]{1,0:T(8,128)}, f32[256,512]{1,0:T(8,128)}, bf16[512,512]{1,0:T(8,128)(2,1)S(1)}) custom-call(s32[1]{0:T(128)S(6)} %copy.51.step, f32[1]{0:T(128)S(6)} %copy.50.push_weight, f32[256,512]{1,0:T(8,128)S(1)} %get-tuple-element.220.own, ...), custom_call_target="tpu_custom_call", output_to_operand_aliasing={{0}: (10, {})} | custom-call | tf_op jit(solution)/shard_map/step_chunk/pallas_call | solution.py:266
  67.7 13.0 %conditional.3 = (bf16[512,512]{1,0:T(8,128)(2,1)}, f32[512,512]{1,0:T(8,128)}, f32[512,512]{1,0:T(8,128)}, bf16[512,512]{1,0:T(8,128)(2,1)}) conditional(s32[]{:T(128)} %bitcast, (bf16[512,512]{1,0:T(8,128)(2,1)S(1)}, f32[1]{0:T(128)}, f32[1]{0:T(128)}, f32[256,512]{1,0:T(8,128)}, f32[256,512]{1,0:T(8,128)}, ...), branch_computations={%region_5.0_spmd, %region_6.0_spmd, %region_7.0_spmd, %region_8.0_... | conditional | bytes 2097224 | solution.py:373
  67.7 0.1 collective-permute-start.14
  67.8 4.5 %mix_chunk.10 = (f32[512,512]{1,0:T(8,128)}, f32[512,512]{1,0:T(8,128)}, bf16[512,512]{1,0:T(8,128)(2,1)}) custom-call(f32[1]{0:T(128)} %get-tuple-element.127.push_weight, f32[1]{0:T(128)} %get-tuple-element.128.other_weight, f32[256,512]{1,0:T(8,128)} %get-tuple-element.129.halfway, f32[256,512]{1,0:T(8,128)} %get-tuple-element.130.first, ...), custom_call_target="tpu_custom_call" | custom-call | tf_op jit(solution)/shard_map/cond/branch_4_fun/mix_chunk/pallas_call | solution.py:318
  72.3 8.3 %collective-permute-done.14 = bf16[512,512]{1,0:T(8,128)(2,1)} collective-permute-done((bf16[512,512]{1,0:T(8,128)(2,1)S(1)}, bf16[512,512]{1,0:T(8,128)(2,1)}, u32[]{:S(2)}, u32[]{:S(2)}) %collective-permute-start.14) | collective-permute-done | bytes 524320 | tf_op jit(solution)/shard_map/cond/branch_4_fun/ppermute | solution.py:352
  80.7 3.9 %mix_chunk.11 = (f32[512,512]{1,0:T(8,128)}, f32[512,512]{1,0:T(8,128)}, bf16[512,512]{1,0:T(8,128)(2,1)}) custom-call(f32[1]{0:T(128)S(6)} %copy.50.push_weight, f32[1]{0:T(128)} %get-tuple-element.213.other_weight, f32[256,512]{1,0:T(8,128)} %get-tuple-element.225.halfway, ...), custom_call_target="tpu_custom_call", output_to_operand_aliasing={{0}: (5, {}), {1}: (6, {}), {2}: (7, {})} | custom-call | tf_op jit(solution)/shard_map/mix_chunk/pallas_call | solution.py:318
  (1 shorter events, 0.0 us)
Async XLA Ops:
  2.7 3.7 %collective-permute-start.15 = (bf16[512,512]{1,0:T(8,128)(2,1)S(1)}, bf16[512,512]{1,0:T(8,128)(2,1)S(1)}, u32[]{:S(2)}, u32[]{:S(2)}) collective-permute-start(bf16[512,512]{1,0:T(8,128)(2,1)S(1)} %other_blocks.2), channel_id=1, source_target_pairs={{0,1},{1,0},{2,3},{3,2},{4,5},{5,4},{6,7},{7,6},{8,9},{9,8},{10,11... | collective-permute-start | bytes 1572872 | tf_op jit(solution)/shard_map/ppermute | solution.py:348
  6.4 10.5 %collective-permute-start.16 = (bf16[1536,512]{1,0:T(8,128)(2,1)S(1)}, bf16[1536,512]{1,0:T(8,128)(2,1)S(1)}, u32[]{:S(2)}, u32[]{:S(2)}) collective-permute-start(bf16[1536,512]{1,0:T(8,128)(2,1)S(1)} %other_blocks.3), channel_id=1, source_target_pairs={{0,1},{1,0},{2,3},{3,2},{4,5},{5,4},{6,7},{7,6},{8,9},{9,8},{10,11... | collective-permute-start | bytes 4718600 | tf_op jit(solution)/shard_map/ppermute | solution.py:348
  9.1 15.7 %collective-permute-start.17 = (bf16[256,512]{1,0:T(8,128)(2,1)S(1)}, bf16[256,512]{1,0:T(8,128)(2,1)S(1)}, u32[]{:S(2)}, u32[]{:S(2)}) collective-permute-start(bf16[256,512]{1,0:T(8,128)(2,1)S(1)} %get-tuple-element.192), channel_id=1, source_target_pairs={{0,2},{1,3},{2,4},{3,5},{4,6},{5,7},{6,0},{7,1},{8,10},{9,11},{10,... | collective-permute-start | bytes 786440 | tf_op jit(solution)/shard_map/ppermute | solution.py:339
  12.4 18.9 %collective-permute-start.18 = (bf16[256,512]{1,0:T(8,128)(2,1)S(1)}, bf16[256,512]{1,0:T(8,128)(2,1)S(1)}, u32[]{:S(2)}, u32[]{:S(2)}) collective-permute-start(bf16[256,512]{1,0:T(8,128)(2,1)S(1)} %get-tuple-element.201), channel_id=1, source_target_pairs={{0,6},{1,7},{2,0},{3,1},{4,2},{5,3},{6,4},{7,5},{8,14},{9,15},{10,... | collective-permute-start | bytes 786440 | tf_op jit(solution)/shard_map/ppermute | solution.py:344
  20.5 22.4 %collective-permute-start.21 = (bf16[256,512]{1,0:T(8,128)(2,1)S(1)}, bf16[256,512]{1,0:T(8,128)(2,1)S(1)}, u32[]{:S(2)}, u32[]{:S(2)}) collective-permute-start(bf16[256,512]{1,0:T(8,128)(2,1)S(1)} %get-tuple-element.204), channel_id=1, source_target_pairs={{0,2},{1,3},{2,4},{3,5},{4,6},{5,7},{6,0},{7,1},{8,10},{9,11},{10,... | collective-permute-start | bytes 786440 | tf_op jit(solution)/shard_map/ppermute | solution.py:339
  22.0 21.0 %collective-permute-start.22 = (bf16[256,512]{1,0:T(8,128)(2,1)S(1)}, bf16[256,512]{1,0:T(8,128)(2,1)S(1)}, u32[]{:S(2)}, u32[]{:S(2)}) collective-permute-start(bf16[256,512]{1,0:T(8,128)(2,1)S(1)} %get-tuple-element.205), channel_id=1, source_target_pairs={{0,6},{1,7},{2,0},{3,1},{4,2},{5,3},{6,4},{7,5},{8,14},{9,15},{10,... | collective-permute-start | bytes 786440 | tf_op jit(solution)/shard_map/ppermute | solution.py:344
  31.3 17.2 %collective-permute-start.19 = (bf16[128,512]{1,0:T(8,128)(2,1)S(1)}, bf16[128,512]{1,0:T(8,128)(2,1)S(1)}, u32[]{:S(2)}, u32[]{:S(2)}) collective-permute-start(bf16[128,512]{1,0:T(8,128)(2,1)S(1)} %get-tuple-element.202), channel_id=1, source_target_pairs={{0,2},{1,3},{2,4},{3,5},{4,6},{5,7},{6,0},{7,1},{8,10},{9,11},{10,... | collective-permute-start | bytes 393224 | tf_op jit(solution)/shard_map/ppermute | solution.py:339
  35.4 13.2 %collective-permute-start.20 = (bf16[128,512]{1,0:T(8,128)(2,1)S(1)}, bf16[128,512]{1,0:T(8,128)(2,1)S(1)}, u32[]{:S(2)}, u32[]{:S(2)}) collective-permute-start(bf16[128,512]{1,0:T(8,128)(2,1)S(1)} %get-tuple-element.203), channel_id=1, source_target_pairs={{0,6},{1,7},{2,0},{3,1},{4,2},{5,3},{6,4},{7,5},{8,14},{9,15},{10,... | collective-permute-start | bytes 393224 | tf_op jit(solution)/shard_map/ppermute | solution.py:344
  43.0 23.2 %collective-permute-start.23 = (bf16[128,512]{1,0:T(8,128)(2,1)S(1)}, bf16[128,512]{1,0:T(8,128)(2,1)S(1)}, u32[]{:S(2)}, u32[]{:S(2)}) collective-permute-start(bf16[128,512]{1,0:T(8,128)(2,1)S(1)} %get-tuple-element.210.refs_0_), channel_id=1, source_target_pairs={{0,2},{1,3},{2,4},{3,5},{4,6},{5,7},{6,0},{7,1},{8,10},{9,11},{10,... | collective-permute-start | bytes 393224 | tf_op jit(solution)/shard_map/ppermute | solution.py:339
  43.7 22.6 %collective-permute-start.24 = (bf16[128,512]{1,0:T(8,128)(2,1)S(1)}, bf16[128,512]{1,0:T(8,128)(2,1)S(1)}, u32[]{:S(2)}, u32[]{:S(2)}) collective-permute-start(bf16[128,512]{1,0:T(8,128)(2,1)S(1)} %get-tuple-element.211.refs_1_), channel_id=1, source_target_pairs={{0,6},{1,7},{2,0},{3,1},{4,2},{5,3},{6,4},{7,5},{8,14},{9,15},{10,... | collective-permute-start | bytes 393224 | tf_op jit(solution)/shard_map/ppermute | solution.py:344
  50.2 14.0 %collective-permute-start.8 = (bf16[512,512]{1,0:T(8,128)(2,1)S(1)}, bf16[512,512]{1,0:T(8,128)(2,1)}, u32[]{:S(2)}, u32[]{:S(2)}) collective-permute-start(bf16[512,512]{1,0:T(8,128)(2,1)S(1)} %get-tuple-element.88), channel_id=1, source_target_pairs={{0,128},{8,136},{16,144},{24,152},{32,160},{40,168},{48,176},{56,1... | collective-permute-start | bytes 1572872 | tf_op jit(solution)/shard_map/cond/branch_4_fun/ppermute | solution.py:352
  50.9 13.3 %collective-permute-start.9 = (f32[1]{0:T(128)}, f32[1]{0:T(128)}, u32[]{:S(2)}, u32[]{:S(2)}) collective-permute-start(f32[1]{0:T(128)} %get-tuple-element.89), channel_id=1, source_target_pairs={{0,128},{8,136},{16,144},{24,152},{32,160},{40,168},{48,176},{56,1... | collective-permute-start | bytes 20 | tf_op jit(solution)/shard_map/cond/branch_4_fun/ppermute | solution.py:352
  67.7 13.0 %collective-permute-start.14 = (bf16[512,512]{1,0:T(8,128)(2,1)S(1)}, bf16[512,512]{1,0:T(8,128)(2,1)}, u32[]{:S(2)}, u32[]{:S(2)}) collective-permute-start(bf16[512,512]{1,0:T(8,128)(2,1)S(1)} %get-tuple-element.126), channel_id=1, source_target_pairs={{0,128},{8,136},{16,144},{24,152},{32,160},{40,168},{48,176},{56,1... | collective-permute-start | bytes 1572872 | tf_op jit(solution)/shard_map/cond/branch_4_fun/ppermute | solution.py:352

commit v2 on v1

v2 whole, which is shorter than its diff:
```python
import math
from functools import partial

import jax
import jax.numpy as jnp
from jax import lax
from jax.experimental import pallas as pl
from jax.experimental.pallas import tpu as pltpu
from jax.sharding import PartitionSpec as P

BETA_ONE = 0.9
BETA_TWO = 0.95
LEARN_RATE = 0.01
DECAY_RATE = 0.1
EPSILON = 1e-08

F32 = jnp.float32
BF16 = jnp.bfloat16
HBM = pl.BlockSpec(memory_space=pltpu.HBM)
SMEM = pl.BlockSpec(memory_space=pltpu.SMEM)
VMEM = pl.BlockSpec(memory_space=pltpu.VMEM)
PARAMS = pltpu.CompilerParams(vmem_limit_bytes=16 * 1024 * 1024)
SMALL = pl.CostEstimate(flops=0, bytes_accessed=0, transcendentals=0)
CHUNKS = ((0, 320), (320, 192))
PARTS = 4
TAIL = 16


def shape(dtype, *sizes):
    return pltpu.VMEM(sizes, dtype)


def in_hbm(array):
    return pltpu.with_memory_space_constraint(array, pltpu.HBM)


def product(x, g):
    return lax.dot_general(x, g, (((0,), (0,)), ((), ())), preferred_element_type=F32)


def first_column(me, ahead, other, width, groups):
    group, core = lax.shift_right_logical(me[0], 1), lax.bitwise_and(me[0], 1)
    low = (2 * lax.rem(group + ahead % groups, groups) + (1 - core if other else core)) * width
    return pl.multiple_of(low, width)


def row_copies(source, columns, held, sems, first):
    part = source.shape[0] // PARTS
    return [
        pltpu.make_async_copy(source.at[pl.ds(i * part, part), columns], held.at[pl.ds(i * part, part)], sems.at[first + i])
        for i in range(PARTS)
    ]


def start(copies):
    for copy in copies:
        copy.start()


def wait(copies):
    for copy in copies:
        copy.wait()


def first_kernel(me, x, g, out, g_held, x_held, sems):
    width, columns = out.shape
    groups = x.shape[1] // (2 * width)
    g_copies = row_copies(g, pl.ds(0, columns), g_held, sems, 0)
    x_copies = row_copies(x, pl.ds(first_column(me, 2, True, width, groups), width), x_held, sems, PARTS)
    start(g_copies)
    start(x_copies)
    wait(g_copies)
    wait(x_copies)
    out[...] = product(x_held[...], g_held[...]).astype(BF16)


def first_block(me, x, g, width):
    tokens, columns = g.shape
    return pl.pallas_call(
        first_kernel,
        in_specs=[SMEM, HBM, HBM],
        out_specs=[VMEM] * 2,
        out_shape=[shape(BF16, width, columns), shape(BF16, tokens, columns)],
        scratch_shapes=[pltpu.VMEM((tokens, width), BF16), pltpu.SemaphoreType.DMA((2 * PARTS,))],
        compiler_params=PARAMS,
        cost_estimate=SMALL,
        name="first_block",
    )(me, x, g)


def others_kernel(me, x, g, out, far, near, x_held, sems):
    width = far.shape[1]
    groups = x.shape[1] // (2 * width)

    def block(ahead, other, held, number):
        low = first_column(me, ahead, other, width, groups)
        return row_copies(x, pl.ds(low, width), held, sems, PARTS * number)

    aheads = (1, -1, 0)
    theirs = [block(ahead, True, x_held.at[k], k) for k, ahead in enumerate(aheads)]
    own = [block(2, False, far, 3)] + [block(ahead, False, near.at[k], 4 + k) for k, ahead in enumerate(aheads)]
    start(theirs[0])
    start(theirs[1])
    for k in range(3):
        wait(theirs[k])
        start(theirs[2] if k == 0 else own[0] if k == 1 else own[1])
        out[pl.ds(k * width, width)] = product(x_held[k], g[...]).astype(BF16)
    start(own[2])
    start(own[3])
    for copies in own:
        wait(copies)


def other_blocks(me, x, g, width):
    tokens, columns = g.shape
    return pl.pallas_call(
        others_kernel,
        in_specs=[SMEM, HBM, VMEM],
        out_specs=[VMEM] * 3,
        out_shape=[shape(BF16, 3 * width, columns), shape(BF16, tokens, width), shape(BF16, 3, tokens, width)],
        scratch_shapes=[pltpu.VMEM((3, tokens, width), BF16), pltpu.SemaphoreType.DMA((7 * PARTS,))],
        compiler_params=PARAMS,
        cost_estimate=SMALL,
        name="other_blocks",
    )(me, x, g)


def far_kernel(x, g, got, *outs):
    total = product(x[...], g[...]) + got[...].astype(F32)
    for k, (low, rows) in enumerate(CHUNKS):
        half = rows // 2
        outs[2 * k][...] = total[low : low + half].astype(BF16)
        outs[2 * k + 1][...] = total[low + half : low + rows].astype(BF16)


def far_block(x, g, got):
    columns = got.shape[1]
    return pl.pallas_call(
        far_kernel,
        in_specs=[VMEM] * 3,
        out_specs=[VMEM] * 4,
        out_shape=[shape(BF16, rows // 2, columns) for _, rows in CHUNKS for _ in range(2)],
        compiler_params=PARAMS,
        cost_estimate=SMALL,
        name="far_block",
    )(x, g, got)


def near_kernel(x, g, got, far_up, far_down, *outs):
    b_up, b_down, rest_up, rest_down, c_up_1, c_down_1, c_up_2, c_down_2, own_1, own_2 = outs
    width = got.shape[0] // 3
    (low_1, rows_1), (low_2, rows_2) = CHUNKS
    half_1, half_2 = rows_1 // 2, rows_2 // 2

    def total(k):
        return product(x[k], g[...]) + got[pl.ds(k * width, width)].astype(F32)

    def plain(values, chunk_1, chunk_2, far, b, rest):
        b[:half_2] = far[...]
        b[half_2:] = values[chunk_1 : chunk_1 + half_1].astype(BF16)
        rest[...] = values[chunk_2 : chunk_2 + half_2].astype(BF16)

    above = total(0)
    plain(above, low_1 + half_1, low_2 + half_2, far_up, b_up, rest_up)
    c_up_1[...] = above[low_1 : low_1 + half_1]
    c_up_2[...] = above[low_2 : low_2 + half_2]
    below = total(1)
    plain(below, low_1, low_2, far_down, b_down, rest_down)
    c_down_1[...] = below[low_1 + half_1 : low_1 + rows_1]
    c_down_2[...] = below[low_2 + half_2 : low_2 + rows_2]
    own = total(2)
    own_1[...] = own[low_1 : low_1 + rows_1]
    own_2[...] = own[low_2 : low_2 + rows_2]


def near_blocks(x, g, got, far_up, far_down):
    columns = g.shape[1]
    (_, rows_1), (_, rows_2) = CHUNKS
    half_1, half_2 = rows_1 // 2, rows_2 // 2
    outs = [shape(BF16, half_2 + half_1, columns)] * 2 + [shape(BF16, half_2, columns)] * 2
    outs += [shape(F32, half_1, columns)] * 2 + [shape(F32, half_2, columns)] * 2
    outs += [shape(F32, rows_1, columns), jax.ShapeDtypeStruct((rows_2, columns), F32)]
    return pl.pallas_call(
        near_kernel,
        in_specs=[VMEM] * 5,
        out_specs=[VMEM] * len(outs),
        out_shape=outs,
        compiler_params=PARAMS,
        cost_estimate=SMALL,
        name="near_blocks",
    )(x, g, got, far_up, far_down)


def add_kernel(low, count, up, got_up, down, got_down, *rest):
    more, outs = rest[:count], rest[-2:]
    half = up.shape[0]
    for mine, got, out in ((up, got_up, outs[0]), (down, got_down, outs[1])):
        out[:half] = (mine[...] + got[pl.ds(low, half)].astype(F32)).astype(BF16)
    for value, out in zip(more, outs):
        out[half:] = value[...]


def add_far(low, up, got_up, down, got_down, more=(), earlier=()):
    rows = up.shape[0] + (more[0].shape[0] if more else 0)
    return pl.pallas_call(
        partial(add_kernel, low, len(more)),
        in_specs=[VMEM] * (4 + len(more)) + [HBM] * len(earlier),
        out_specs=[VMEM] * 2,
        out_shape=[shape(BF16, rows, up.shape[1])] * 2,
        compiler_params=PARAMS,
        cost_estimate=SMALL,
        name="add_far",
    )(up, got_up, down, got_down, *more, *earlier)


def fetch_kernel(places, *refs):
    count = len(places)
    copies = []
    for i, (start, rows) in enumerate(places):
        source, held, sems = refs[i], refs[count + i], refs[2 * count]
        part = rows // 2
        for k in range(2):
            copies.append(
                pltpu.make_async_copy(
                    source.at[pl.ds(start + k * part, part)], held.at[pl.ds(k * part, part)], sems.at[2 * i + k]
                )
            )
            copies[-1].start()
    for copy in copies:
        copy.wait()


def fetch(places, *arrays):
    return pl.pallas_call(
        partial(fetch_kernel, places),
        in_specs=[HBM] * len(arrays),
        out_specs=[VMEM] * len(arrays),
        out_shape=[shape(a.dtype, rows, a.shape[1]) for a, (_, rows) in zip(arrays, places)],
        scratch_shapes=[pltpu.SemaphoreType.DMA((2 * len(arrays),))],
        compiler_params=PARAMS,
        cost_estimate=SMALL,
        name="fetch",
    )(*arrays)


def step_kernel(first_row, places, kept, step, push_weight, own, c_up, c_down, *refs):
    count = 1 + max(at for at, _, _ in places)
    b_ups, b_downs = refs[:count], refs[count : 2 * count]
    master, one, two = refs[2 * count : 2 * count + 3]
    if kept:
        second_out, halfway_made, first_made, send, second_made, sems = refs[-6:]
        away = [(second_made, second_out, first_row)]
    else:
        second_out, halfway_out, first_out, send, second_made, halfway_made, first_made, sems = refs[-8:]
        away = [(second_made, second_out, first_row), (halfway_made, halfway_out, 0), (first_made, first_out, 0)]
    copies = []
    rows, columns = own.shape
    line = lax.broadcasted_iota(jnp.int32, (TAIL, columns), 0)
    left = jnp.full((TAIL, columns), push_weight[0], F32)
    high = left.astype(BF16).astype(F32)
    middle = (left - high).astype(BF16).astype(F32)
    low = left - high - middle
    parts = jnp.where(line == 0, high, jnp.where(line == 1, middle, jnp.where(line == 2, low, 0.0)))
    send[pl.ds(2 * rows, TAIL)] = parts.astype(BF16)
    half = rows // 2
    row = (1, columns)
    number = jnp.full(row, step[0] + 1, jnp.int32).astype(F32)
    scale_one = 1.0 / (1.0 - jnp.exp(number * math.log(BETA_ONE)))
    scale_two = 1.0 / (1.0 - jnp.exp(number * math.log(BETA_TWO)))
    decay = DECAY_RATE / jnp.full(row, push_weight[0], F32)
    for low, c, b_pieces in ((0, c_up, b_downs), (half, c_down, b_ups)):
        to = 0
        for which, b_low, size in places:
            at = pl.ds(low + to, size)
            far = b_pieces[which][pl.ds(b_low, size)].astype(F32)
            gradient = own[at] + (c[pl.ds(to, size)].astype(F32) + far)
            first = BETA_ONE * one[at] + (1.0 - BETA_ONE) * gradient
            second = BETA_TWO * two[at] + (1.0 - BETA_TWO) * gradient * gradient
            direction = first * scale_one / (jnp.sqrt(second * scale_two) + EPSILON)
            weights = master[at]
            halfway = weights - LEARN_RATE * (direction + weights * decay)
            second_made[at] = second
            halfway_made[at] = halfway
            first_made[at] = first
            send[at] = halfway.astype(BF16)
            send[pl.ds(rows + low + to, size)] = first.astype(BF16)
            to += size
        at = pl.ds(low, half)
        for made, out, place in away:
            copies.append(pltpu.make_async_copy(made.at[at], out.at[pl.ds(place + low, half)], sems.at[len(copies)]))
            copies[-1].start()
    for copy in copies:
        copy.wait()


def step_chunk(first_row, height, places, kept, ins, before=(), earlier=()):
    rows, columns = ins[2].shape
    return pl.pallas_call(
        partial(step_kernel, first_row, places, kept),
        in_specs=[SMEM] * 2 + [VMEM] * (len(ins) - 2) + [HBM] * (len(before) + len(earlier)),
        out_specs=[HBM] + [VMEM if kept else HBM] * 2 + [VMEM],
        out_shape=[pltpu.HBM((height, columns), F32)]
        + [(pltpu.VMEM if kept else pltpu.HBM)((rows, columns), F32)] * 2
        + [shape(BF16, 2 * rows + TAIL, columns)],
        scratch_shapes=[pltpu.VMEM((rows, columns), F32)] * (1 if kept else 3) + [pltpu.SemaphoreType.DMA((6,))],
        input_output_aliases={len(ins): 0} if before else {},
        compiler_params=PARAMS,
        cost_estimate=SMALL,
        name="step_chunk",
    )(*ins, *before, *earlier)


def mixed_scale(push_weight, tail):
    return 1.0 / (0.5 * (push_weight[0] + jnp.sum(tail.astype(F32), axis=0, keepdims=True)))


def mix_kernel(first_row, rows, push_weight, halfway, first, got, *rest):
    master_out, first_out, copy_out, master_new, first_new, copy, in_sems, out_sems = rest[-8:]
    pieces = 4
    part = rows // pieces
    at = [pl.ds(k * part, part) for k in range(pieces)]
    behind = [pl.ds(rows + k * part, part) for k in range(pieces)]
    loads = [
        [
            pltpu.make_async_copy(source.at[at[k]], held.at[at[k]], in_sems.at[2 * k + i])
            for i, (source, held) in enumerate(((halfway, master_new), (first, first_new)))
        ]
        for k in range(pieces)
    ]
    for pair in loads:
        start(pair)
    sends = []
    scale = mixed_scale(push_weight, got[pl.ds(2 * rows, TAIL)])
    for k in range(pieces):
        wait(loads[k])
        mixed = 0.5 * (master_new[at[k]] + got[at[k]].astype(F32))
        master_new[at[k]] = mixed
        copy[at[k]] = (mixed * scale).astype(BF16)
        first_new[at[k]] = 0.5 * (first_new[at[k]] + got[behind[k]].astype(F32))
        to = pl.ds(first_row + k * part, part)
        sends.append(
            [
                pltpu.make_async_copy(made.at[at[k]], out.at[to], out_sems.at[3 * k + i])
                for i, (made, out) in enumerate(((master_new, master_out), (first_new, first_out), (copy, copy_out)))
            ]
        )
        start(sends[k])
    for three in sends:
        wait(three)


def mix_chunk(first_row, rows, height, push_weight, halfway, first, got, before=()):
    columns = halfway.shape[1]
    ins = (push_weight, in_hbm(halfway), in_hbm(first), got)
    return pl.pallas_call(
        partial(mix_kernel, first_row, rows),
        in_specs=[SMEM] + [HBM] * 2 + [VMEM] + [HBM] * len(before),
        out_specs=[HBM] * 3,
        out_shape=[pltpu.HBM((height, columns), F32)] * 2 + [pltpu.HBM((height, columns), BF16)],
        scratch_shapes=[
            pltpu.VMEM((rows, columns), F32),
            pltpu.VMEM((rows, columns), F32),
            pltpu.VMEM((rows, columns), BF16),
            pltpu.SemaphoreType.DMA((8,)),
            pltpu.SemaphoreType.DMA((12,)),
        ],
        input_output_aliases={len(ins) + i: i for i in range(len(before))},
        compiler_params=PARAMS,
        cost_estimate=SMALL,
        name="mix_chunk",
    )(*ins, *before)


def last_kernel(first_row, rows, push_weight, halfway, first, got, *rest):
    master_out, first_out, copy_out, master_new, first_new, copy, sems = rest[-7:]
    pieces = 2
    part = rows // pieces
    scale = mixed_scale(push_weight, got[pl.ds(2 * rows, TAIL)])
    sends = []
    for k in range(pieces):
        at, to = pl.ds(k * part, part), pl.ds(first_row + k * part, part)
        mixed = 0.5 * (halfway[at] + got[at].astype(F32))
        master_new[at] = mixed
        copy[at] = (mixed * scale).astype(BF16)
        first_new[at] = 0.5 * (first[at] + got[pl.ds(rows + k * part, part)].astype(F32))
        sends += [
            pltpu.make_async_copy(made.at[at], out.at[to], sems.at[3 * k + i])
            for i, (made, out) in enumerate(((master_new, master_out), (first_new, first_out), (copy, copy_out)))
        ]
        start(sends[3 * k :])
    wait(sends)


def last_mix(first_row, rows, height, push_weight, halfway, first, got, before):
    columns = halfway.shape[1]
    ins = (push_weight, halfway, first, got)
    return pl.pallas_call(
        partial(last_kernel, first_row, rows),
        in_specs=[SMEM] + [VMEM] * 3 + [HBM] * len(before),
        out_specs=[HBM] * 3,
        out_shape=[pltpu.HBM((height, columns), F32)] * 2 + [pltpu.HBM((height, columns), BF16)],
        scratch_shapes=[
            pltpu.VMEM((rows, columns), F32),
            pltpu.VMEM((rows, columns), F32),
            pltpu.VMEM((rows, columns), BF16),
            pltpu.SemaphoreType.DMA((6,)),
        ],
        input_output_aliases={len(ins) + i: i for i in range(len(before))},
        compiler_params=PARAMS,
        cost_estimate=SMALL,
        name="last_mix",
    )(*ins, *before)


def pass_kernel(*refs):
    refs[-1][0] = jnp.int32(0)


def passed(*arrays):
    return pl.pallas_call(
        pass_kernel,
        in_specs=[HBM] * len(arrays),
        out_specs=[HBM] * len(arrays),
        out_shape=[pltpu.HBM(a.shape, a.dtype) for a in arrays],
        scratch_shapes=[pltpu.SMEM((1,), jnp.int32)],
        input_output_aliases={i: i for i in range(len(arrays))},
        compiler_params=PARAMS,
        cost_estimate=SMALL,
        name="passed",
    )(*arrays)


def up_z(block):
    count = lax.axis_size("fsdp")
    return lax.ppermute(block, "fsdp", [(i, (i + 2) % count) for i in range(count)])


def down_z(block):
    count = lax.axis_size("fsdp")
    return lax.ppermute(block, "fsdp", [(i, (i - 2) % count) for i in range(count)])


def other_core(block):
    return lax.ppermute(block, "fsdp", [(i, i ^ 1) for i in range(lax.axis_size("fsdp"))])


def from_partner(block, bit):
    return lax.ppermute(block, "rep", [(i, i ^ (1 << bit)) for i in range(lax.axis_size("rep"))])


def after(value, *earlier):
    return lax.optimization_barrier((value, *earlier))[0]


def exchanges(height, bit, push_weight, step_index, send_1, halfway_1, first_1, second, rest_up, rest_down, own_2, *state):
    (low_2, rows_2), half_2 = CHUNKS[1], CHUNKS[1][1] // 2
    got_1 = from_partner(send_1, bit)
    got_rest = up_z(rest_up), down_z(rest_down)
    *state_2, own_2 = fetch(((low_2, rows_2),) * 3 + ((0, rows_2),), *(in_hbm(v) for v in (*state, own_2)))
    second, halfway_2, first_2, send_2 = step_chunk(
        low_2,
        height,
        ((0, half_2, half_2),),
        True,
        (step_index, push_weight, own_2, *got_rest, *got_rest, *state_2),
        (second,),
    )
    got_2 = from_partner(send_2, bit)
    other_weight = from_partner(push_weight, bit)
    mixed = mix_chunk(*CHUNKS[0], height, push_weight, halfway_1, first_1, got_1)
    return (other_weight, second, *last_mix(*CHUNKS[1], height, push_weight, halfway_2, first_2, got_2, mixed))


def on_device(activations, cotangent, master, moment_one, moment_two, push_weight, step_index):
    x, g, state = in_hbm(activations), in_hbm(cotangent), [in_hbm(v[0]) for v in (master, moment_one, moment_two)]
    height = master.shape[1]
    bits = lax.axis_size("rep").bit_length() - 1

    me = jnp.full((1,), lax.axis_index("fsdp"), jnp.int32)
    (low_1, rows_1), (low_2, rows_2) = CHUNKS
    half_1, half_2 = rows_1 // 2, rows_2 // 2
    out_far, g_held = first_block(me, x, g, height)
    got_far = other_core(out_far)
    out_near, x_far, x_near = other_blocks(me, x, g_held, height)
    got_near = other_core(after(out_near, got_far))
    a_up_1, a_down_1, a_up_2, a_down_2 = far_block(x_far, g_held, got_far)
    got_a_up, got_a_down = up_z(a_up_1), down_z(a_down_1)
    b_up, b_down, *later, c_up_1, c_down_1, c_up_2, c_down_2, own_1, own_2 = near_blocks(
        x_near, g_held, got_near, a_up_2, a_down_2
    )
    got_b = up_z(b_up), down_z(b_down)
    state_1 = fetch([(low_1, rows_1)] * 3, *(after(v, b_up) for v in state))
    c_up_1, c_down_1 = add_far(0, c_up_1, got_a_up, c_down_1, got_a_down)
    got_c = up_z(c_up_1), down_z(c_down_1)
    rest = add_far(0, c_up_2, got_b[0], c_down_2, got_b[1], later, (*got_c, state_1[0]))
    second, *made_1 = step_chunk(
        low_1, height, ((0, half_2, half_1),), False, (step_index, push_weight, own_1, *got_c, *got_b, *state_1)
    )
    other_weight, *made = lax.switch(
        lax.rem(step_index[0], bits),
        [partial(exchanges, height, bit) for bit in range(bits)],
        push_weight,
        step_index,
        made_1[2],
        *made_1[:2],
        second,
        *rest,
        own_2,
        *state,
    )
    second, mixed, first, copy = passed(*made)
    weight_new = 0.5 * (push_weight + other_weight)
    return (mixed[None], first[None], second[None], weight_new, copy[None])


def solution(mesh):
    placed = (
        P(("rep", "fsdp"), None),
        P(("rep", "fsdp"), None),
        P("rep", "fsdp", None),
        P("rep", "fsdp", None),
        P("rep", "fsdp", None),
        P("rep"),
        P(),
    )
    return jax.shard_map(
        on_device,
        mesh=mesh,
        in_specs=placed,
        out_specs=(
            P("rep", "fsdp", None),
            P("rep", "fsdp", None),
            P("rep", "fsdp", None),
            P("rep"),
            P("rep", "fsdp", None),
        ),
        check_vma=False,
    )
```

time: 86.7 us -> 77 us (0.89)
  the two profiles are of different devices: /device:TPU:6 before, /device:TPU:56 now
where the time goes in v2:
time: 77 us; the launch traced here: 78 us
  waiting for transfers between devices  27.9 us (36%)
  starting transfers between devices  25.3 us (33%)
  Pallas kernels  20.8 us (27%)
  between operations  3.79 us (5%)
    ppermute x4, waiting for transfers between devices, up_z(): lax.ppermute(block, 'fsdp', [(i, (i + 2) % count) for i in range(count)])  12.8 us
    ppermute x4, starting transfers between devices, up_z(): lax.ppermute(block, 'fsdp', [(i, (i + 2) % count) for i in range(count)])  9.78 us
    ppermute x4, waiting for transfers between devices, down_z(): lax.ppermute(block, 'fsdp', [(i, (i - 2) % count) for i in range(count)])  9.59 us
    ppermute x4, starting transfers between devices, down_z(): lax.ppermute(block, 'fsdp', [(i, (i - 2) % count) for i in range(count)])  8.27 us
    ppermute x3, starting transfers between devices, from_partner(): lax.ppermute(block, 'rep', [(i, i ^ 1 << bit) for i in range(lax.axis_siz...  6.57 us
    ppermute x3, waiting for transfers between devices, from_partner(): lax.ppermute(block, 'rep', [(i, i ^ 1 << bit) for i in range(lax.axis_siz...  5.5 us
    pallas_call x1, Pallas kernels, other_blocks(): pl.pallas_call(others_kernel, in_specs=[SMEM, HBM, VMEM], out_specs=[VMEM...  4.32 us
    pallas_call x2, Pallas kernels, step_chunk(): pl.pallas_call(partial(step_kernel, first_row, places, kept), in_specs=[S...  3.72 us
  transfers between devices with their start and end apart: 13, of which 6 were waited for; matrix products, arithmetic and copies ran while one was open for 0% of the time, Pallas kernels for 22%

profile of v2, /device:TPU:56, one launch (start us, length us, event | category | flops | bytes accessed | tf_op | source)
XLA Modules:
  0.0 78.0 jit_solution(16705524341658624175)
XLA Ops:
  0.6 2.1 %first_block.1 = (bf16[512,512]{1,0:T(8,128)(2,1)S(1)}, bf16[704,512]{1,0:T(8,128)(2,1)S(1)}) custom-call(s32[1]{0:T(128)} %bitcast.4.me, bf16[704,4096]{1,0:T(8,128)(2,1)} %x.3, bf16[704,512]{1,0:T(8,128)(2,1)} %g.1), custom_call_target="tpu_custom_call" | custom-call | tf_op jit(solution)/shard_map/first_block/pallas_call | solution.py:79
  2.7 0.1 collective-permute-start.25
  2.8 4.3 %other_blocks.1 = (bf16[1536,512]{1,0:T(8,128)(2,1)S(1)}, bf16[704,512]{1,0:T(8,128)(2,1)S(1)}, bf16[3,704,512]{2,1,0:T(8,128)(2,1)S(1)}) custom-call(s32[1]{0:T(128)} %bitcast.4.me, bf16[704,4096]{1,0:T(8,128)(2,1)} %x.3, bf16[704,512]{1,0:T(8,128)(2,1)S(1)} %get-tuple-element.298.g), custom_call_target="tpu_custom_call" | custom-call | tf_op jit(solution)/shard_map/other_blocks/pallas_call | solution.py:116
  7.2 0.0 collective-permute-done.25.got
  7.2 0.6 collective-permute-start.26
  7.7 0.6 far_block.1
  8.4 3.3 %collective-permute-start.29 = (bf16[160,512]{1,0:T(8,128)(2,1)S(1)}, bf16[160,512]{1,0:T(8,128)(2,1)S(1)}, u32[]{:S(2)}, u32[]{:S(2)}) collective-permute-start(bf16[160,512]{1,0:T(8,128)(2,1)S(1)} %get-tuple-element.314), channel_id=1, source_target_pairs={{0,2},{1,3},{2,4},{3,5},{4,6},{5,7},{6,0},{7,1},{8,10},{9,11},{10,... | collective-permute-start | bytes 491528 | tf_op jit(solution)/shard_map/ppermute | solution.py:435
  11.7 2.2 %collective-permute-start.30 = (bf16[160,512]{1,0:T(8,128)(2,1)S(1)}, bf16[160,512]{1,0:T(8,128)(2,1)S(1)}, u32[]{:S(2)}, u32[]{:S(2)}) collective-permute-start(bf16[160,512]{1,0:T(8,128)(2,1)S(1)} %get-tuple-element.316), channel_id=1, source_target_pairs={{0,6},{1,7},{2,0},{3,1},{4,2},{5,3},{6,4},{7,5},{8,14},{9,15},{10,... | collective-permute-start | bytes 491528 | tf_op jit(solution)/shard_map/ppermute | solution.py:440
  13.9 0.0 collective-permute-done.26.got
  13.9 2.2 %near_blocks.1 = (bf16[256,512]{1,0:T(8,128)(2,1)S(1)}, bf16[256,512]{1,0:T(8,128)(2,1)S(1)}, bf16[96,512]{1,0:T(8,128)(2,1)S(1)}, bf16[96,512]{1,0:T(8,128)(2,1...) custom-call(bf16[3,704,512]{2,1,0:T(8,128)(2,1)S(1)} %get-tuple-elem, ...), custom_call_target="tpu_custom_call" | custom-call | tf_op jit(solution)/shard_map/near_blocks/pallas_call | solution.py:183
  16.1 1.4 %collective-permute-start.27 = (bf16[256,512]{1,0:T(8,128)(2,1)S(1)}, bf16[256,512]{1,0:T(8,128)(2,1)S(1)}, u32[]{:S(2)}, u32[]{:S(2)}) collective-permute-start(bf16[256,512]{1,0:T(8,128)(2,1)S(1)} %get-tuple-element.308), channel_id=1, source_target_pairs={{0,2},{1,3},{2,4},{3,5},{4,6},{5,7},{6,0},{7,1},{8,10},{9,11},{10,... | collective-permute-start | bytes 786440 | tf_op jit(solution)/shard_map/ppermute | solution.py:435
  17.5 2.8 %collective-permute-start.28 = (bf16[256,512]{1,0:T(8,128)(2,1)S(1)}, bf16[256,512]{1,0:T(8,128)(2,1)S(1)}, u32[]{:S(2)}, u32[]{:S(2)}) collective-permute-start(bf16[256,512]{1,0:T(8,128)(2,1)S(1)} %get-tuple-element.310), channel_id=1, source_target_pairs={{0,6},{1,7},{2,0},{3,1},{4,2},{5,3},{6,4},{7,5},{8,14},{9,15},{10,... | collective-permute-start | bytes 786440 | tf_op jit(solution)/shard_map/ppermute | solution.py:440
  20.2 2.6 %collective-permute-done.29.got_up = bf16[160,512]{1,0:T(8,128)(2,1)S(1)} collective-permute-done((bf16[160,512]{1,0:T(8,128)(2,1)S(1)}, bf16[160,512]{1,0:T(8,128)(2,1)S(1)}, u32[]{:S(2)}, u32[]{:S(2)}) %collective-permute-start.29) | collective-permute-done | bytes 163872 | tf_op jit(solution)/shard_map/ppermute | solution.py:435
  22.9 0.0 collective-permute-done.30.got_down
  22.9 0.1 add_far.2
  22.9 2.4 %collective-permute-start.31 = (bf16[160,512]{1,0:T(8,128)(2,1)S(1)}, bf16[160,512]{1,0:T(8,128)(2,1)S(1)}, u32[]{:S(2)}, u32[]{:S(2)}) collective-permute-start(bf16[160,512]{1,0:T(8,128)(2,1)S(1)} %get-tuple-element.317), channel_id=1, source_target_pairs={{0,2},{1,3},{2,4},{3,5},{4,6},{5,7},{6,0},{7,1},{8,10},{9,11},{10,... | collective-permute-start | bytes 491528 | tf_op jit(solution)/shard_map/ppermute | solution.py:435
  25.3 1.8 %collective-permute-start.32 = (bf16[160,512]{1,0:T(8,128)(2,1)S(1)}, bf16[160,512]{1,0:T(8,128)(2,1)S(1)}, u32[]{:S(2)}, u32[]{:S(2)}) collective-permute-start(bf16[160,512]{1,0:T(8,128)(2,1)S(1)} %get-tuple-element.318), channel_id=1, source_target_pairs={{0,6},{1,7},{2,0},{3,1},{4,2},{5,3},{6,4},{7,5},{8,14},{9,15},{10,... | collective-permute-start | bytes 491528 | tf_op jit(solution)/shard_map/ppermute | solution.py:440
  28.4 1.5 %fetch.11 = (f32[320,512]{1,0:T(8,128)S(1)}, f32[320,512]{1,0:T(8,128)S(1)}, f32[320,512]{1,0:T(8,128)S(1)}) custom-call(f32[512,512]{1,0:T(8,128)} %bitcast.9, f32[512,512]{1,0:T(8,128)} %bitcast.15, f32[512,512]{1,0:T(8,128)} %bitcast.21), custom_call_target="tpu_custom_call" | custom-call | tf_op jit(solution)/shard_map/fetch/pallas_call | solution.py:234
  30.0 4.9 %collective-permute-done.31.rest_2_.c_up = bf16[160,512]{1,0:T(8,128)(2,1)S(1)} collective-permute-done((bf16[160,512]{1,0:T(8,128)(2,1)S(1)}, bf16[160,512]{1,0:T(8,128)(2,1)S(1)}, u32[]{:S(2)}, u32[]{:S(2)}) %collective-permute-start.31) | collective-permute-done | bytes 163872 | tf_op jit(solution)/shard_map/ppermute | solution.py:435
  34.9 7.2 %collective-permute-done.32.rest_3_.c_down = bf16[160,512]{1,0:T(8,128)(2,1)S(1)} collective-permute-done((bf16[160,512]{1,0:T(8,128)(2,1)S(1)}, bf16[160,512]{1,0:T(8,128)(2,1)S(1)}, u32[]{:S(2)}, u32[]{:S(2)}) %collective-permute-start.32) | collective-permute-done | bytes 163872 | tf_op jit(solution)/shard_map/ppermute | solution.py:440
  42.1 0.0 collective-permute-done.27.got_up.refs_0_
  42.1 0.0 collective-permute-done.28.got_down.refs_1_
  42.1 1.6 %step_chunk.11 = (f32[512,512]{1,0:T(8,128)}, f32[320,512]{1,0:T(8,128)}, f32[320,512]{1,0:T(8,128)}, bf16[656,512]{1,0:T(8,128)(2,1)S(1)}) custom-call(s32[1]{0:T(128)S(6)} %copy.86.step, f32[1]{0:T(128)S(6)} %copy.85.push_weight, f32[320,512]{1,0:T(8,128)S(1)} %get-tuple-element.325.own, bf16[160,512]{1,0:T(8,128)(2,1)S(1)} %collective-permute-done.31.rest_2_.c_up, ...), custom_call_target="tpu_custom_call" | custom-call | tf_op jit(solution)/shard_map/step_chunk/pallas_call | solution.py:298
  43.7 32.5 %conditional.1 = (f32[1]{0:T(128)}, f32[512,512]{1,0:T(8,128)}, f32[512,512]{1,0:T(8,128)}, f32[512,512]{1,0:T(8,128)}, bf16[512,512]{1,0:T(8,128)(2,1)}) conditional(s32[]{:T(128)} %bitcast, (f32[1]{0:T(128)}, f32[512,512]{1,0:T(8,128)}, f32[512,512]{1,0:T(8,128)}, f32[512,512]{1,0:T(8,128)}, f32[192,512]{1,0:T(8,128)}, ...), branch_computations={%region_0.0_spmd, %region_1.0_spmd, %region_2.0_spmd, %region_3.0_... | conditional | bytes 5898496 | solution.py:499
  44.0 3.0 %collective-permute-start.19 = (bf16[656,512]{1,0:T(8,128)(2,1)S(1)}, bf16[656,512]{1,0:T(8,128)(2,1)S(1)}, u32[]{:S(2)}, u32[]{:S(2)}) collective-permute-start(bf16[656,512]{1,0:T(8,128)(2,1)S(1)} %get-tuple-element.217), channel_id=1, source_target_pairs={{0,64},{8,72},{16,80},{24,88},{32,96},{40,104},{48,112},{56,120},{... | collective-permute-start | bytes 2015240 | tf_op jit(solution)/shard_map/cond/branch_3_fun/ppermute | solution.py:448
  46.9 2.7 %collective-permute-start.16 = (bf16[192,512]{1,0:T(8,128)(2,1)S(1)}, bf16[192,512]{1,0:T(8,128)(2,1)S(1)}, u32[]{:S(2)}, u32[]{:S(2)}) collective-permute-start(bf16[192,512]{1,0:T(8,128)(2,1)S(1)} %get-tuple-element.205), channel_id=1, source_target_pairs={{0,2},{1,3},{2,4},{3,5},{4,6},{5,7},{6,0},{7,1},{8,10},{9,11},{10,... | collective-permute-start | bytes 589832 | tf_op jit(solution)/shard_map/cond/branch_3_fun/ppermute | solution.py:435
  49.6 1.5 %collective-permute-start.17 = (bf16[192,512]{1,0:T(8,128)(2,1)S(1)}, bf16[192,512]{1,0:T(8,128)(2,1)S(1)}, u32[]{:S(2)}, u32[]{:S(2)}) collective-permute-start(bf16[192,512]{1,0:T(8,128)(2,1)S(1)} %get-tuple-element.206), channel_id=1, source_target_pairs={{0,6},{1,7},{2,0},{3,1},{4,2},{5,3},{6,4},{7,5},{8,14},{9,15},{10,... | collective-permute-start | bytes 589832 | tf_op jit(solution)/shard_map/cond/branch_3_fun/ppermute | solution.py:440
  51.1 1.5 %fetch.9 = (f32[192,512]{1,0:T(8,128)S(1)}, f32[192,512]{1,0:T(8,128)S(1)}, f32[192,512]{1,0:T(8,128)S(1)}, f32[192,512]{1,0:T(8,128)S(1)}) custom-call(f32[512,512]{1,0:T(8,128)} %get-tuple-element.200.refs_0_, f32[512,512]{1,0:T(8,128)} %get-tuple-element.201.refs_1_, f32[512,512]{1,0:T(8,128)} %get-tuple-element.202.refs_2_, ...), custom_call_target="tpu_custom_call" | custom-call | tf_op jit(solution)/shard_map/cond/branch_3_fun/fetch/pallas_call | solution.py:234
  52.6 5.3 %collective-permute-done.16.c_up.refs_0_ = bf16[192,512]{1,0:T(8,128)(2,1)S(1)} collective-permute-done((bf16[192,512]{1,0:T(8,128)(2,1)S(1)}, bf16[192,512]{1,0:T(8,128)(2,1)S(1)}, u32[]{:S(2)}, u32[]{:S(2)}) %collective-permute-start.16) | collective-permute-done | bytes 196640 | tf_op jit(solution)/shard_map/cond/branch_3_fun/ppermute | solution.py:435
  57.9 2.4 %collective-permute-done.17.c_down.refs_1_ = bf16[192,512]{1,0:T(8,128)(2,1)S(1)} collective-permute-done((bf16[192,512]{1,0:T(8,128)(2,1)S(1)}, bf16[192,512]{1,0:T(8,128)(2,1)S(1)}, u32[]{:S(2)}, u32[]{:S(2)}) %collective-permute-start.17) | collective-permute-done | bytes 196640 | tf_op jit(solution)/shard_map/cond/branch_3_fun/ppermute | solution.py:440
  60.2 2.2 %step_chunk.9 = (f32[512,512]{1,0:T(8,128)}, f32[192,512]{1,0:T(8,128)S(1)}, f32[192,512]{1,0:T(8,128)S(1)}, bf16[400,512]{1,0:T(8,128)(2,1)S(1)}) custom-call(s32[1]{0:T(128)} %get-tuple-element.199.step, f32[1]{0:T(128)} %get-tuple-element.198.push_weight, f32[192,512]{1,0:T(8,128)S(1)} %get-tuple-element.204.own, ...), custom_call_target="tpu_custom_call", output_to_operand_aliasing={{0}: (10, {})} | custom-call | tf_op jit(solution)/shard_map/cond/branch_3_fun/step_chunk/pallas_call | solution.py:298
  62.4 0.5 collective-permute-start.18
  63.0 3.1 %collective-permute-start.15 = (f32[1]{0:T(128)}, f32[1]{0:T(128)}, u32[]{:S(2)}, u32[]{:S(2)}) collective-permute-start(f32[1]{0:T(128)} %get-tuple-element.198.push_weight), channel_id=1, source_target_pairs={{0,64},{8,72},{16,80},{24,88},{32,96},{40,104},{48,112},{56,120},{... | collective-permute-start | bytes 20 | tf_op jit(solution)/shard_map/cond/branch_3_fun/ppermute | solution.py:448
  66.0 0.0 collective-permute-done.19.got
  66.0 3.0 %mix_chunk.8 = (f32[512,512]{1,0:T(8,128)}, f32[512,512]{1,0:T(8,128)}, bf16[512,512]{1,0:T(8,128)(2,1)}) custom-call(f32[1]{0:T(128)} %get-tuple-element.198.push_weight, f32[320,512]{1,0:T(8,128)} %get-tuple-element.215.halfway, f32[320,512]{1,0:T(8,128)} %get-tuple-element.216.first, bf16[656,512]{1,0:T(8,128)(2,1)S(1)} %collective-permute-done.19.got), custom_call_target="tpu_custom_call" | custom-call | tf_op jit(solution)/shard_map/cond/branch_3_fun/mix_chunk/pallas_call | solution.py:355
  69.1 5.5 %collective-permute-done.18.got = bf16[400,512]{1,0:T(8,128)(2,1)S(1)} collective-permute-done((bf16[400,512]{1,0:T(8,128)(2,1)S(1)}, bf16[400,512]{1,0:T(8,128)(2,1)S(1)}, u32[]{:S(2)}, u32[]{:S(2)}) %collective-permute-start.18) | collective-permute-done | bytes 409632 | tf_op jit(solution)/shard_map/cond/branch_3_fun/ppermute | solution.py:448
  74.6 1.7 %last_mix.8 = (f32[512,512]{1,0:T(8,128)}, f32[512,512]{1,0:T(8,128)}, bf16[512,512]{1,0:T(8,128)(2,1)}) custom-call(f32[1]{0:T(128)} %get-tuple-element.198.push_weight, f32[192,512]{1,0:T(8,128)S(1)} %get-tuple-element.212.halfway, f32[192,512]{1,0:T(8,128)S(1)} %get-tuple-element.213.first, ...), custom_call_target="tpu_custom_call", output_to_operand_aliasing={{0}: (4, {}), {1}: (5, {}), {2}: (6, {})} | custom-call | tf_op jit(solution)/shard_map/cond/branch_3_fun/last_mix/pallas_call | solution.py:397
  76.2 0.0 collective-permute-done.15
  (2 shorter events, 0.1 us)
Async XLA Ops:
  2.7 4.4 %collective-permute-start.25 = (bf16[512,512]{1,0:T(8,128)(2,1)S(1)}, bf16[512,512]{1,0:T(8,128)(2,1)S(1)}, u32[]{:S(2)}, u32[]{:S(2)}) collective-permute-start(bf16[512,512]{1,0:T(8,128)(2,1)S(1)} %get-tuple-element.301), channel_id=1, source_target_pairs={{0,1},{1,0},{2,3},{3,2},{4,5},{5,4},{6,7},{7,6},{8,9},{9,8},{10,11... | collective-permute-start | bytes 1572872 | tf_op jit(solution)/shard_map/ppermute | solution.py:444
  7.2 6.8 %collective-permute-start.26 = (bf16[1536,512]{1,0:T(8,128)(2,1)S(1)}, bf16[1536,512]{1,0:T(8,128)(2,1)S(1)}, u32[]{:S(2)}, u32[]{:S(2)}) collective-permute-start(bf16[1536,512]{1,0:T(8,128)(2,1)S(1)} %get-tuple-element.302), channel_id=1, source_target_pairs={{0,1},{1,0},{2,3},{3,2},{4,5},{5,4},{6,7},{7,6},{8,9},{9,8},{10,11... | collective-permute-start | bytes 4718600 | tf_op jit(solution)/shard_map/ppermute | solution.py:444
  8.4 14.5 %collective-permute-start.29 = (bf16[160,512]{1,0:T(8,128)(2,1)S(1)}, bf16[160,512]{1,0:T(8,128)(2,1)S(1)}, u32[]{:S(2)}, u32[]{:S(2)}) collective-permute-start(bf16[160,512]{1,0:T(8,128)(2,1)S(1)} %get-tuple-element.314), channel_id=1, source_target_pairs={{0,2},{1,3},{2,4},{3,5},{4,6},{5,7},{6,0},{7,1},{8,10},{9,11},{10,... | collective-permute-start | bytes 491528 | tf_op jit(solution)/shard_map/ppermute | solution.py:435
  11.7 11.2 %collective-permute-start.30 = (bf16[160,512]{1,0:T(8,128)(2,1)S(1)}, bf16[160,512]{1,0:T(8,128)(2,1)S(1)}, u32[]{:S(2)}, u32[]{:S(2)}) collective-permute-start(bf16[160,512]{1,0:T(8,128)(2,1)S(1)} %get-tuple-element.316), channel_id=1, source_target_pairs={{0,6},{1,7},{2,0},{3,1},{4,2},{5,3},{6,4},{7,5},{8,14},{9,15},{10,... | collective-permute-start | bytes 491528 | tf_op jit(solution)/shard_map/ppermute | solution.py:440
  16.1 26.0 %collective-permute-start.27 = (bf16[256,512]{1,0:T(8,128)(2,1)S(1)}, bf16[256,512]{1,0:T(8,128)(2,1)S(1)}, u32[]{:S(2)}, u32[]{:S(2)}) collective-permute-start(bf16[256,512]{1,0:T(8,128)(2,1)S(1)} %get-tuple-element.308), channel_id=1, source_target_pairs={{0,2},{1,3},{2,4},{3,5},{4,6},{5,7},{6,0},{7,1},{8,10},{9,11},{10,... | collective-permute-start | bytes 786440 | tf_op jit(solution)/shard_map/ppermute | solution.py:435
  17.5 24.6 %collective-permute-start.28 = (bf16[256,512]{1,0:T(8,128)(2,1)S(1)}, bf16[256,512]{1,0:T(8,128)(2,1)S(1)}, u32[]{:S(2)}, u32[]{:S(2)}) collective-permute-start(bf16[256,512]{1,0:T(8,128)(2,1)S(1)} %get-tuple-element.310), channel_id=1, source_target_pairs={{0,6},{1,7},{2,0},{3,1},{4,2},{5,3},{6,4},{7,5},{8,14},{9,15},{10,... | collective-permute-start | bytes 786440 | tf_op jit(solution)/shard_map/ppermute | solution.py:440
  22.9 12.0 %collective-permute-start.31 = (bf16[160,512]{1,0:T(8,128)(2,1)S(1)}, bf16[160,512]{1,0:T(8,128)(2,1)S(1)}, u32[]{:S(2)}, u32[]{:S(2)}) collective-permute-start(bf16[160,512]{1,0:T(8,128)(2,1)S(1)} %get-tuple-element.317), channel_id=1, source_target_pairs={{0,2},{1,3},{2,4},{3,5},{4,6},{5,7},{6,0},{7,1},{8,10},{9,11},{10,... | collective-permute-start | bytes 491528 | tf_op jit(solution)/shard_map/ppermute | solution.py:435
  25.3 16.8 %collective-permute-start.32 = (bf16[160,512]{1,0:T(8,128)(2,1)S(1)}, bf16[160,512]{1,0:T(8,128)(2,1)S(1)}, u32[]{:S(2)}, u32[]{:S(2)}) collective-permute-start(bf16[160,512]{1,0:T(8,128)(2,1)S(1)} %get-tuple-element.318), channel_id=1, source_target_pairs={{0,6},{1,7},{2,0},{3,1},{4,2},{5,3},{6,4},{7,5},{8,14},{9,15},{10,... | collective-permute-start | bytes 491528 | tf_op jit(solution)/shard_map/ppermute | solution.py:440
  44.0 22.1 %collective-permute-start.19 = (bf16[656,512]{1,0:T(8,128)(2,1)S(1)}, bf16[656,512]{1,0:T(8,128)(2,1)S(1)}, u32[]{:S(2)}, u32[]{:S(2)}) collective-permute-start(bf16[656,512]{1,0:T(8,128)(2,1)S(1)} %get-tuple-element.217), channel_id=1, source_target_pairs={{0,64},{8,72},{16,80},{24,88},{32,96},{40,104},{48,112},{56,120},{... | collective-permute-start | bytes 2015240 | tf_op jit(solution)/shard_map/cond/branch_3_fun/ppermute | solution.py:448
  46.9 10.9 %collective-permute-start.16 = (bf16[192,512]{1,0:T(8,128)(2,1)S(1)}, bf16[192,512]{1,0:T(8,128)(2,1)S(1)}, u32[]{:S(2)}, u32[]{:S(2)}) collective-permute-start(bf16[192,512]{1,0:T(8,128)(2,1)S(1)} %get-tuple-element.205), channel_id=1, source_target_pairs={{0,2},{1,3},{2,4},{3,5},{4,6},{5,7},{6,0},{7,1},{8,10},{9,11},{10,... | collective-permute-start | bytes 589832 | tf_op jit(solution)/shard_map/cond/branch_3_fun/ppermute | solution.py:435
  49.6 10.6 %collective-permute-start.17 = (bf16[192,512]{1,0:T(8,128)(2,1)S(1)}, bf16[192,512]{1,0:T(8,128)(2,1)S(1)}, u32[]{:S(2)}, u32[]{:S(2)}) collective-permute-start(bf16[192,512]{1,0:T(8,128)(2,1)S(1)} %get-tuple-element.206), channel_id=1, source_target_pairs={{0,6},{1,7},{2,0},{3,1},{4,2},{5,3},{6,4},{7,5},{8,14},{9,15},{10,... | collective-permute-start | bytes 589832 | tf_op jit(solution)/shard_map/cond/branch_3_fun/ppermute | solution.py:440
  62.4 12.2 %collective-permute-start.18 = (bf16[400,512]{1,0:T(8,128)(2,1)S(1)}, bf16[400,512]{1,0:T(8,128)(2,1)S(1)}, u32[]{:S(2)}, u32[]{:S(2)}) collective-permute-start(bf16[400,512]{1,0:T(8,128)(2,1)S(1)} %get-tuple-element.214), channel_id=1, source_target_pairs={{0,64},{8,72},{16,80},{24,88},{32,96},{40,104},{48,112},{56,120},{... | collective-permute-start | bytes 1228808 | tf_op jit(solution)/shard_map/cond/branch_3_fun/ppermute | solution.py:448
  63.0 13.3 %collective-permute-start.15 = (f32[1]{0:T(128)}, f32[1]{0:T(128)}, u32[]{:S(2)}, u32[]{:S(2)}) collective-permute-start(f32[1]{0:T(128)} %get-tuple-element.198.push_weight), channel_id=1, source_target_pairs={{0,64},{8,72},{16,80},{24,88},{32,96},{40,104},{48,112},{56,120},{... | collective-permute-start | bytes 20 | tf_op jit(solution)/shard_map/cond/branch_3_fun/ppermute | solution.py:448

commit v3 on v2

--- a/solution.py
+++ b/solution.py
@@ -243,16 +243,11 @@
     )(*arrays)
 
 
-def step_kernel(first_row, places, kept, step, push_weight, own, c_up, c_down, *refs):
-    count = 1 + max(at for at, _, _ in places)
-    b_ups, b_downs = refs[:count], refs[count : 2 * count]
+def step_kernel(first_row, places, step, push_weight, own, c_up, c_down, *refs):
+    count = max(at for at, _, _ in places)
+    b_ups, b_downs = (c_up, *refs[:count]), (c_down, *refs[count : 2 * count])
     master, one, two = refs[2 * count : 2 * count + 3]
-    if kept:
-        second_out, halfway_made, first_made, send, second_made, sems = refs[-6:]
-        away = [(second_made, second_out, first_row)]
-    else:
-        second_out, halfway_out, first_out, send, second_made, halfway_made, first_made, sems = refs[-8:]
-        away = [(second_made, second_out, first_row), (halfway_made, halfway_out, 0), (first_made, first_out, 0)]
+    second_out, halfway_out, first_out, send, second_made, sems = refs[-6:]
     copies = []
     rows, columns = own.shape
     line = lax.broadcasted_iota(jnp.int32, (TAIL, columns), 0)
@@ -280,29 +275,30 @@
             weights = master[at]
             halfway = weights - LEARN_RATE * (direction + weights * decay)
             second_made[at] = second
-            halfway_made[at] = halfway
-            first_made[at] = first
+            halfway_out[at] = halfway
+            first_out[at] = first
             send[at] = halfway.astype(BF16)
             send[pl.ds(rows + low + to, size)] = first.astype(BF16)
             to += size
         at = pl.ds(low, half)
-        for made, out, place in away:
-            copies.append(pltpu.make_async_copy(made.at[at], out.at[pl.ds(place + low, half)], sems.at[len(copies)]))
-            copies[-1].start()
+        copies.append(
+            pltpu.make_async_copy(second_made.at[at], second_out.at[pl.ds(first_row + low, half)], sems.at[len(copies)])
+        )
+        copies[-1].start()
     for copy in copies:
         copy.wait()
 
 
-def step_chunk(first_row, height, places, kept, ins, before=(), earlier=()):
+def step_chunk(first_row, height, places, ins, before=(), earlier=()):
     rows, columns = ins[2].shape
     return pl.pallas_call(
-        partial(step_kernel, first_row, places, kept),
+        partial(step_kernel, first_row, places),
         in_specs=[SMEM] * 2 + [VMEM] * (len(ins) - 2) + [HBM] * (len(before) + len(earlier)),
-        out_specs=[HBM] + [VMEM if kept else HBM] * 2 + [VMEM],
+        out_specs=[HBM] + [VMEM] * 3,
         out_shape=[pltpu.HBM((height, columns), F32)]
-        + [(pltpu.VMEM if kept else pltpu.HBM)((rows, columns), F32)] * 2
+        + [shape(F32, rows, columns)] * 2
         + [shape(BF16, 2 * rows + TAIL, columns)],
-        scratch_shapes=[pltpu.VMEM((rows, columns), F32)] * (1 if kept else 3) + [pltpu.SemaphoreType.DMA((6,))],
+        scratch_shapes=[pltpu.VMEM((rows, columns), F32), pltpu.SemaphoreType.DMA((2,))],
         input_output_aliases={len(ins): 0} if before else {},
         compiler_params=PARAMS,
         cost_estimate=SMALL,
@@ -315,63 +311,6 @@
 
 
 def mix_kernel(first_row, rows, push_weight, halfway, first, got, *rest):
-    master_out, first_out, copy_out, master_new, first_new, copy, in_sems, out_sems = rest[-8:]
-    pieces = 4
-    part = rows // pieces
-    at = [pl.ds(k * part, part) for k in range(pieces)]
-    behind = [pl.ds(rows + k * part, part) for k in range(pieces)]
-    loads = [
-        [
-            pltpu.make_async_copy(source.at[at[k]], held.at[at[k]], in_sems.at[2 * k + i])
-            for i, (source, held) in enumerate(((halfway, master_new), (first, first_new)))
-        ]
-        for k in range(pieces)
-    ]
-    for pair in loads:
-        start(pair)
-    sends = []
-    scale = mixed_scale(push_weight, got[pl.ds(2 * rows, TAIL)])
-    for k in range(pieces):
-        wait(loads[k])
-        mixed = 0.5 * (master_new[at[k]] + got[at[k]].astype(F32))
-        master_new[at[k]] = mixed
-        copy[at[k]] = (mixed * scale).astype(BF16)
-        first_new[at[k]] = 0.5 * (first_new[at[k]] + got[behind[k]].astype(F32))
-        to = pl.ds(first_row + k * part, part)
-        sends.append(
-            [
-                pltpu.make_async_copy(made.at[at[k]], out.at[to], out_sems.at[3 * k + i])
-                for i, (made, out) in enumerate(((master_new, master_out), (first_new, first_out), (copy, copy_out)))
-            ]
-        )
-        start(sends[k])
-    for three in sends:
-        wait(three)
-
-
-def mix_chunk(first_row, rows, height, push_weight, halfway, first, got, before=()):
-    columns = halfway.shape[1]
-    ins = (push_weight, in_hbm(halfway), in_hbm(first), got)
-    return pl.pallas_call(
-        partial(mix_kernel, first_row, rows),
-        in_specs=[SMEM] + [HBM] * 2 + [VMEM] + [HBM] * len(before),
-        out_specs=[HBM] * 3,
-        out_shape=[pltpu.HBM((height, columns), F32)] * 2 + [pltpu.HBM((height, columns), BF16)],
-        scratch_shapes=[
-            pltpu.VMEM((rows, columns), F32),
-            pltpu.VMEM((rows, columns), F32),
-            pltpu.VMEM((rows, columns), BF16),
-            pltpu.SemaphoreType.DMA((8,)),
-            pltpu.SemaphoreType.DMA((12,)),
-        ],
-        input_output_aliases={len(ins) + i: i for i in range(len(before))},
-        compiler_params=PARAMS,
-        cost_estimate=SMALL,
-        name="mix_chunk",
-    )(*ins, *before)
-
-
-def last_kernel(first_row, rows, push_weight, halfway, first, got, *rest):
     master_out, first_out, copy_out, master_new, first_new, copy, sems = rest[-7:]
     pieces = 2
     part = rows // pieces
@@ -391,11 +330,11 @@
     wait(sends)
 
 
-def last_mix(first_row, rows, height, push_weight, halfway, first, got, before):
+def mix_chunk(first_row, rows, height, push_weight, halfway, first, got, before=()):
     columns = halfway.shape[1]
     ins = (push_weight, halfway, first, got)
     return pl.pallas_call(
-        partial(last_kernel, first_row, rows),
+        partial(mix_kernel, first_row, rows),
         in_specs=[SMEM] + [VMEM] * 3 + [HBM] * len(before),
         out_specs=[HBM] * 3,
         out_shape=[pltpu.HBM((height, columns), F32)] * 2 + [pltpu.HBM((height, columns), BF16)],
@@ -408,7 +347,7 @@
         input_output_aliases={len(ins) + i: i for i in range(len(before))},
         compiler_params=PARAMS,
         cost_estimate=SMALL,
-        name="last_mix",
+        name="mix_chunk",
     )(*ins, *before)
 
 
@@ -461,14 +400,13 @@
         low_2,
         height,
         ((0, half_2, half_2),),
-        True,
-        (step_index, push_weight, own_2, *got_rest, *got_rest, *state_2),
+        (step_index, push_weight, own_2, *got_rest, *state_2),
         (second,),
     )
     got_2 = from_partner(send_2, bit)
     other_weight = from_partner(push_weight, bit)
     mixed = mix_chunk(*CHUNKS[0], height, push_weight, halfway_1, first_1, got_1)
-    return (other_weight, second, *last_mix(*CHUNKS[1], height, push_weight, halfway_2, first_2, got_2, mixed))
+    return (other_weight, second, *mix_chunk(*CHUNKS[1], height, push_weight, halfway_2, first_2, got_2, mixed))
 
 
 def on_device(activations, cotangent, master, moment_one, moment_two, push_weight, step_index):
@@ -494,7 +432,7 @@
     got_c = up_z(c_up_1), down_z(c_down_1)
     rest = add_far(0, c_up_2, got_b[0], c_down_2, got_b[1], later, (*got_c, state_1[0]))
     second, *made_1 = step_chunk(
-        low_1, height, ((0, half_2, half_1),), False, (step_index, push_weight, own_1, *got_c, *got_b, *state_1)
+        low_1, height, ((1, half_2, half_1),), (step_index, push_weight, own_1, *got_c, *got_b, *state_1)
     )
     other_weight, *made = lax.switch(
         lax.rem(step_index[0], bits),

time: 77 us -> 77.8 us (1.010); the launches traced: 78 us -> 77.3 us
  Pallas kernels: 20.8 us -> 19 us
  waiting for transfers between devices: 27.9 us -> 29.1 us
    pallas_call x4, Pallas kernels: 8.41 us -> 6.68 us  [the longest x2 3.57 us: mix_chunk(): pl.pallas_call(partial(mix_kernel, first_row, rows), in_specs=[SMEM] + [V...]
    ppermute x3, waiting for transfers between devices: 5.5 us -> 6.75 us  [from_partner(): lax.ppermute(block, 'rep', [(i, i ^ 1 << bit) for i in range(lax.axis_siz...]
  transfers between devices with their start and end apart: 13 -> 13, of which waited for: 6 -> 6; matrix products, arithmetic and copies ran while one was open for 0% -> 0% of each run, Pallas kernels for 22% -> 21%
where the time goes in v3:
time: 77.8 us; the launch traced here: 77.3 us
  waiting for transfers between devices  29.1 us (37%)
  starting transfers between devices  25 us (32%)
  Pallas kernels  19 us (24%)
  between operations  3.78 us (5%)
    ppermute x4, waiting for transfers between devices, up_z(): lax.ppermute(block, 'fsdp', [(i, (i + 2) % count) for i in range(count)])  13.4 us
    ppermute x4, starting transfers between devices, up_z(): lax.ppermute(block, 'fsdp', [(i, (i + 2) % count) for i in range(count)])  9.95 us
    ppermute x4, waiting for transfers between devices, down_z(): lax.ppermute(block, 'fsdp', [(i, (i - 2) % count) for i in range(count)])  8.96 us
    ppermute x4, starting transfers between devices, down_z(): lax.ppermute(block, 'fsdp', [(i, (i - 2) % count) for i in range(count)])  8.1 us
    ppermute x3, waiting for transfers between devices, from_partner(): lax.ppermute(block, 'rep', [(i, i ^ 1 << bit) for i in range(lax.axis_siz...  6.75 us
    ppermute x3, starting transfers between devices, from_partner(): lax.ppermute(block, 'rep', [(i, i ^ 1 << bit) for i in range(lax.axis_siz...  6.3 us
    pallas_call x1, Pallas kernels, other_blocks(): pl.pallas_call(others_kernel, in_specs=[SMEM, HBM, VMEM], out_specs=[VMEM...  4.32 us
    pallas_call x2, Pallas kernels, mix_chunk(): pl.pallas_call(partial(mix_kernel, first_row, rows), in_specs=[SMEM] + [V...  3.57 us
  transfers between devices with their start and end apart: 13, of which 6 were waited for; matrix products, arithmetic and copies ran while one was open for 0% of the time, Pallas kernels for 21%

profile of v3, /device:TPU:56, one launch (start us, length us, event | category | flops | bytes accessed | tf_op | source)
XLA Modules:
  0.0 77.3 jit_solution(2455700943419191301)
XLA Ops:
  0.6 2.1 %first_block.1 = (bf16[512,512]{1,0:T(8,128)(2,1)S(1)}, bf16[704,512]{1,0:T(8,128)(2,1)S(1)}) custom-call(s32[1]{0:T(128)} %bitcast.4.me, bf16[704,4096]{1,0:T(8,128)(2,1)} %x.3, bf16[704,512]{1,0:T(8,128)(2,1)} %g.1), custom_call_target="tpu_custom_call" | custom-call | tf_op jit(solution)/shard_map/first_block/pallas_call | solution.py:79
  2.7 0.1 collective-permute-start.25
  2.8 4.3 %other_blocks.1 = (bf16[1536,512]{1,0:T(8,128)(2,1)S(1)}, bf16[704,512]{1,0:T(8,128)(2,1)S(1)}, bf16[3,704,512]{2,1,0:T(8,128)(2,1)S(1)}) custom-call(s32[1]{0:T(128)} %bitcast.4.me, bf16[704,4096]{1,0:T(8,128)(2,1)} %x.3, bf16[704,512]{1,0:T(8,128)(2,1)S(1)} %get-tuple-element.298.g), custom_call_target="tpu_custom_call" | custom-call | tf_op jit(solution)/shard_map/other_blocks/pallas_call | solution.py:116
  7.2 0.0 collective-permute-done.25.got
  7.2 0.6 collective-permute-start.26
  7.7 0.6 far_block.1
  8.4 3.3 %collective-permute-start.29 = (bf16[160,512]{1,0:T(8,128)(2,1)S(1)}, bf16[160,512]{1,0:T(8,128)(2,1)S(1)}, u32[]{:S(2)}, u32[]{:S(2)}) collective-permute-start(bf16[160,512]{1,0:T(8,128)(2,1)S(1)} %get-tuple-element.314), channel_id=1, source_target_pairs={{0,2},{1,3},{2,4},{3,5},{4,6},{5,7},{6,0},{7,1},{8,10},{9,11},{10,... | collective-permute-start | bytes 491528 | tf_op jit(solution)/shard_map/ppermute | solution.py:374
  11.7 2.2 %collective-permute-start.30 = (bf16[160,512]{1,0:T(8,128)(2,1)S(1)}, bf16[160,512]{1,0:T(8,128)(2,1)S(1)}, u32[]{:S(2)}, u32[]{:S(2)}) collective-permute-start(bf16[160,512]{1,0:T(8,128)(2,1)S(1)} %get-tuple-element.316), channel_id=1, source_target_pairs={{0,6},{1,7},{2,0},{3,1},{4,2},{5,3},{6,4},{7,5},{8,14},{9,15},{10,... | collective-permute-start | bytes 491528 | tf_op jit(solution)/shard_map/ppermute | solution.py:379
  13.9 0.0 collective-permute-done.26.got
  13.9 2.2 %near_blocks.1 = (bf16[256,512]{1,0:T(8,128)(2,1)S(1)}, bf16[256,512]{1,0:T(8,128)(2,1)S(1)}, bf16[96,512]{1,0:T(8,128)(2,1)S(1)}, bf16[96,512]{1,0:T(8,128)(2,1...) custom-call(bf16[3,704,512]{2,1,0:T(8,128)(2,1)S(1)} %get-tuple-elem, ...), custom_call_target="tpu_custom_call" | custom-call | tf_op jit(solution)/shard_map/near_blocks/pallas_call | solution.py:183
  16.1 1.4 %collective-permute-start.27 = (bf16[256,512]{1,0:T(8,128)(2,1)S(1)}, bf16[256,512]{1,0:T(8,128)(2,1)S(1)}, u32[]{:S(2)}, u32[]{:S(2)}) collective-permute-start(bf16[256,512]{1,0:T(8,128)(2,1)S(1)} %get-tuple-element.308), channel_id=1, source_target_pairs={{0,2},{1,3},{2,4},{3,5},{4,6},{5,7},{6,0},{7,1},{8,10},{9,11},{10,... | collective-permute-start | bytes 786440 | tf_op jit(solution)/shard_map/ppermute | solution.py:374
  17.5 2.8 %collective-permute-start.28 = (bf16[256,512]{1,0:T(8,128)(2,1)S(1)}, bf16[256,512]{1,0:T(8,128)(2,1)S(1)}, u32[]{:S(2)}, u32[]{:S(2)}) collective-permute-start(bf16[256,512]{1,0:T(8,128)(2,1)S(1)} %get-tuple-element.310), channel_id=1, source_target_pairs={{0,6},{1,7},{2,0},{3,1},{4,2},{5,3},{6,4},{7,5},{8,14},{9,15},{10,... | collective-permute-start | bytes 786440 | tf_op jit(solution)/shard_map/ppermute | solution.py:379
  20.2 2.6 %collective-permute-done.29.got_up = bf16[160,512]{1,0:T(8,128)(2,1)S(1)} collective-permute-done((bf16[160,512]{1,0:T(8,128)(2,1)S(1)}, bf16[160,512]{1,0:T(8,128)(2,1)S(1)}, u32[]{:S(2)}, u32[]{:S(2)}) %collective-permute-start.29) | collective-permute-done | bytes 163872 | tf_op jit(solution)/shard_map/ppermute | solution.py:374
  22.8 0.0 collective-permute-done.30.got_down
  22.9 0.1 add_far.2
  22.9 2.4 %collective-permute-start.31 = (bf16[160,512]{1,0:T(8,128)(2,1)S(1)}, bf16[160,512]{1,0:T(8,128)(2,1)S(1)}, u32[]{:S(2)}, u32[]{:S(2)}) collective-permute-start(bf16[160,512]{1,0:T(8,128)(2,1)S(1)} %get-tuple-element.317), channel_id=1, source_target_pairs={{0,2},{1,3},{2,4},{3,5},{4,6},{5,7},{6,0},{7,1},{8,10},{9,11},{10,... | collective-permute-start | bytes 491528 | tf_op jit(solution)/shard_map/ppermute | solution.py:374
  25.3 1.8 %collective-permute-start.32 = (bf16[160,512]{1,0:T(8,128)(2,1)S(1)}, bf16[160,512]{1,0:T(8,128)(2,1)S(1)}, u32[]{:S(2)}, u32[]{:S(2)}) collective-permute-start(bf16[160,512]{1,0:T(8,128)(2,1)S(1)} %get-tuple-element.318), channel_id=1, source_target_pairs={{0,6},{1,7},{2,0},{3,1},{4,2},{5,3},{6,4},{7,5},{8,14},{9,15},{10,... | collective-permute-start | bytes 491528 | tf_op jit(solution)/shard_map/ppermute | solution.py:379
  28.4 1.5 %fetch.11 = (f32[320,512]{1,0:T(8,128)S(1)}, f32[320,512]{1,0:T(8,128)S(1)}, f32[320,512]{1,0:T(8,128)S(1)}) custom-call(f32[512,512]{1,0:T(8,128)} %bitcast.9, f32[512,512]{1,0:T(8,128)} %bitcast.15, f32[512,512]{1,0:T(8,128)} %bitcast.21), custom_call_target="tpu_custom_call" | custom-call | tf_op jit(solution)/shard_map/fetch/pallas_call | solution.py:234
  30.0 5.3 %collective-permute-done.31.rest_2_.c_up = bf16[160,512]{1,0:T(8,128)(2,1)S(1)} collective-permute-done((bf16[160,512]{1,0:T(8,128)(2,1)S(1)}, bf16[160,512]{1,0:T(8,128)(2,1)S(1)}, u32[]{:S(2)}, u32[]{:S(2)}) %collective-permute-start.31) | collective-permute-done | bytes 163872 | tf_op jit(solution)/shard_map/ppermute | solution.py:374
  35.3 6.8 %collective-permute-done.32.rest_3_.c_down = bf16[160,512]{1,0:T(8,128)(2,1)S(1)} collective-permute-done((bf16[160,512]{1,0:T(8,128)(2,1)S(1)}, bf16[160,512]{1,0:T(8,128)(2,1)S(1)}, u32[]{:S(2)}, u32[]{:S(2)}) %collective-permute-start.32) | collective-permute-done | bytes 163872 | tf_op jit(solution)/shard_map/ppermute | solution.py:379
  42.1 0.0 collective-permute-done.27.got_up.refs_0_
  42.1 0.0 collective-permute-done.28.got_down.refs_1_
  42.1 1.0 %step_chunk.11 = (f32[512,512]{1,0:T(8,128)}, f32[320,512]{1,0:T(8,128)S(1)}, f32[320,512]{1,0:T(8,128)S(1)}, bf16[656,512]{1,0:T(8,128)(2,1)S(1)}) custom-call(s32[1]{0:T(128)S(6)} %copy.86.step, f32[1]{0:T(128)S(6)} %copy.85.push_weight, f32[320,512]{1,0:T(8,128)S(1)} %get-tuple-element.325.own, bf16[160,512]{1,0:T(8,128)(2,1)S(1)} %collective-permute-done.31.rest_2_.c_up, ...), custom_call_target="tpu_custom_call" | custom-call | tf_op jit(solution)/shard_map/step_chunk/pallas_call | solution.py:294
  43.2 32.3 %conditional.1 = (f32[1]{0:T(128)}, f32[512,512]{1,0:T(8,128)}, f32[512,512]{1,0:T(8,128)}, f32[512,512]{1,0:T(8,128)}, bf16[512,512]{1,0:T(8,128)(2,1)}) conditional(s32[]{:T(128)} %bitcast, (f32[1]{0:T(128)}, f32[512,512]{1,0:T(8,128)}, f32[512,512]{1,0:T(8,128)}, f32[512,512]{1,0:T(8,128)}, f32[192,512]{1,0:T(8,128)}, ...), branch_computations={%region_0.0_spmd, %region_1.0_spmd, %region_2.0_spmd, %region_3.0_... | conditional | bytes 5898496 | solution.py:437
  43.4 2.7 %collective-permute-start.19 = (bf16[656,512]{1,0:T(8,128)(2,1)S(1)}, bf16[656,512]{1,0:T(8,128)(2,1)S(1)}, u32[]{:S(2)}, u32[]{:S(2)}) collective-permute-start(bf16[656,512]{1,0:T(8,128)(2,1)S(1)} %get-tuple-element.217), channel_id=1, source_target_pairs={{0,64},{8,72},{16,80},{24,88},{32,96},{40,104},{48,112},{56,120},{... | collective-permute-start | bytes 2015240 | tf_op jit(solution)/shard_map/cond/branch_3_fun/ppermute | solution.py:387
  46.1 2.8 %collective-permute-start.16 = (bf16[192,512]{1,0:T(8,128)(2,1)S(1)}, bf16[192,512]{1,0:T(8,128)(2,1)S(1)}, u32[]{:S(2)}, u32[]{:S(2)}) collective-permute-start(bf16[192,512]{1,0:T(8,128)(2,1)S(1)} %get-tuple-element.205), channel_id=1, source_target_pairs={{0,2},{1,3},{2,4},{3,5},{4,6},{5,7},{6,0},{7,1},{8,10},{9,11},{10,... | collective-permute-start | bytes 589832 | tf_op jit(solution)/shard_map/cond/branch_3_fun/ppermute | solution.py:374
  48.9 1.3 %collective-permute-start.17 = (bf16[192,512]{1,0:T(8,128)(2,1)S(1)}, bf16[192,512]{1,0:T(8,128)(2,1)S(1)}, u32[]{:S(2)}, u32[]{:S(2)}) collective-permute-start(bf16[192,512]{1,0:T(8,128)(2,1)S(1)} %get-tuple-element.206), channel_id=1, source_target_pairs={{0,6},{1,7},{2,0},{3,1},{4,2},{5,3},{6,4},{7,5},{8,14},{9,15},{10,... | collective-permute-start | bytes 589832 | tf_op jit(solution)/shard_map/cond/branch_3_fun/ppermute | solution.py:379
  50.2 1.5 %fetch.9 = (f32[192,512]{1,0:T(8,128)S(1)}, f32[192,512]{1,0:T(8,128)S(1)}, f32[192,512]{1,0:T(8,128)S(1)}, f32[192,512]{1,0:T(8,128)S(1)}) custom-call(f32[512,512]{1,0:T(8,128)} %get-tuple-element.200.refs_0_, f32[512,512]{1,0:T(8,128)} %get-tuple-element.201.refs_1_, f32[512,512]{1,0:T(8,128)} %get-tuple-element.202.refs_2_, ...), custom_call_target="tpu_custom_call" | custom-call | tf_op jit(solution)/shard_map/cond/branch_3_fun/fetch/pallas_call | solution.py:234
  51.8 5.5 %collective-permute-done.16.c_up = bf16[192,512]{1,0:T(8,128)(2,1)S(1)} collective-permute-done((bf16[192,512]{1,0:T(8,128)(2,1)S(1)}, bf16[192,512]{1,0:T(8,128)(2,1)S(1)}, u32[]{:S(2)}, u32[]{:S(2)}) %collective-permute-start.16) | collective-permute-done | bytes 196640 | tf_op jit(solution)/shard_map/cond/branch_3_fun/ppermute | solution.py:374
  57.3 2.1 %collective-permute-done.17.c_down = bf16[192,512]{1,0:T(8,128)(2,1)S(1)} collective-permute-done((bf16[192,512]{1,0:T(8,128)(2,1)S(1)}, bf16[192,512]{1,0:T(8,128)(2,1)S(1)}, u32[]{:S(2)}, u32[]{:S(2)}) %collective-permute-start.17) | collective-permute-done | bytes 196640 | tf_op jit(solution)/shard_map/cond/branch_3_fun/ppermute | solution.py:379
  59.4 2.1 %step_chunk.9 = (f32[512,512]{1,0:T(8,128)}, f32[192,512]{1,0:T(8,128)S(1)}, f32[192,512]{1,0:T(8,128)S(1)}, bf16[400,512]{1,0:T(8,128)(2,1)S(1)}) custom-call(s32[1]{0:T(128)} %get-tuple-element.199.step, f32[1]{0:T(128)} %get-tuple-element.198.push_weight, f32[192,512]{1,0:T(8,128)S(1)} %get-tuple-element.204.own, ...), custom_call_target="tpu_custom_call", output_to_operand_aliasing={{0}: (8, {})} | custom-call | tf_op jit(solution)/shard_map/cond/branch_3_fun/step_chunk/pallas_call | solution.py:294
  61.5 0.8 %collective-permute-start.18 = (bf16[400,512]{1,0:T(8,128)(2,1)S(1)}, bf16[400,512]{1,0:T(8,128)(2,1)S(1)}, u32[]{:S(2)}, u32[]{:S(2)}) collective-permute-start(bf16[400,512]{1,0:T(8,128)(2,1)S(1)} %get-tuple-element.214), channel_id=1, source_target_pairs={{0,64},{8,72},{16,80},{24,88},{32,96},{40,104},{48,112},{56,120},{... | collective-permute-start | bytes 1228808 | tf_op jit(solution)/shard_map/cond/branch_3_fun/ppermute | solution.py:387
  62.3 2.8 %collective-permute-start.15 = (f32[1]{0:T(128)}, f32[1]{0:T(128)}, u32[]{:S(2)}, u32[]{:S(2)}) collective-permute-start(f32[1]{0:T(128)} %get-tuple-element.198.push_weight), channel_id=1, source_target_pairs={{0,64},{8,72},{16,80},{24,88},{32,96},{40,104},{48,112},{56,120},{... | collective-permute-start | bytes 20 | tf_op jit(solution)/shard_map/cond/branch_3_fun/ppermute | solution.py:387
  65.2 0.0 collective-permute-done.19.got
  65.2 1.9 %mix_chunk.16 = (f32[512,512]{1,0:T(8,128)}, f32[512,512]{1,0:T(8,128)}, bf16[512,512]{1,0:T(8,128)(2,1)}) custom-call(f32[1]{0:T(128)} %get-tuple-element.198.push_weight, f32[320,512]{1,0:T(8,128)S(1)} %get-tuple-element.215.halfway, f32[320,512]{1,0:T(8,128)S(1)} %get-tuple-element.216.first, bf16[656,512]{1,0:T(8,128)(2,1)S(1)} %collective-permute-done.19.got), custom_call_target="tpu_custom_call" | custom-call | tf_op jit(solution)/shard_map/cond/branch_3_fun/mix_chunk/pallas_call | solution.py:336
  67.1 6.7 %collective-permute-done.18.got = bf16[400,512]{1,0:T(8,128)(2,1)S(1)} collective-permute-done((bf16[400,512]{1,0:T(8,128)(2,1)S(1)}, bf16[400,512]{1,0:T(8,128)(2,1)S(1)}, u32[]{:S(2)}, u32[]{:S(2)}) %collective-permute-start.18) | collective-permute-done | bytes 409632 | tf_op jit(solution)/shard_map/cond/branch_3_fun/ppermute | solution.py:387
  73.8 1.7 %mix_chunk.17 = (f32[512,512]{1,0:T(8,128)}, f32[512,512]{1,0:T(8,128)}, bf16[512,512]{1,0:T(8,128)(2,1)}) custom-call(f32[1]{0:T(128)} %get-tuple-element.198.push_weight, f32[192,512]{1,0:T(8,128)S(1)} %get-tuple-element.212.halfway, f32[192,512]{1,0:T(8,128)S(1)} %get-tuple-element.213.first, ...), custom_call_target="tpu_custom_call", output_to_operand_aliasing={{0}: (4, {}), {1}: (5, {}), {2}: (6, {})} | custom-call | tf_op jit(solution)/shard_map/cond/branch_3_fun/mix_chunk/pallas_call | solution.py:336
  75.5 0.0 collective-permute-done.15
  (2 shorter events, 0.1 us)
Async XLA Ops:
  2.7 4.4 %collective-permute-start.25 = (bf16[512,512]{1,0:T(8,128)(2,1)S(1)}, bf16[512,512]{1,0:T(8,128)(2,1)S(1)}, u32[]{:S(2)}, u32[]{:S(2)}) collective-permute-start(bf16[512,512]{1,0:T(8,128)(2,1)S(1)} %get-tuple-element.301), channel_id=1, source_target_pairs={{0,1},{1,0},{2,3},{3,2},{4,5},{5,4},{6,7},{7,6},{8,9},{9,8},{10,11... | collective-permute-start | bytes 1572872 | tf_op jit(solution)/shard_map/ppermute | solution.py:383
  7.2 6.8 %collective-permute-start.26 = (bf16[1536,512]{1,0:T(8,128)(2,1)S(1)}, bf16[1536,512]{1,0:T(8,128)(2,1)S(1)}, u32[]{:S(2)}, u32[]{:S(2)}) collective-permute-start(bf16[1536,512]{1,0:T(8,128)(2,1)S(1)} %get-tuple-element.302), channel_id=1, source_target_pairs={{0,1},{1,0},{2,3},{3,2},{4,5},{5,4},{6,7},{7,6},{8,9},{9,8},{10,11... | collective-permute-start | bytes 4718600 | tf_op jit(solution)/shard_map/ppermute | solution.py:383
  8.4 14.5 %collective-permute-start.29 = (bf16[160,512]{1,0:T(8,128)(2,1)S(1)}, bf16[160,512]{1,0:T(8,128)(2,1)S(1)}, u32[]{:S(2)}, u32[]{:S(2)}) collective-permute-start(bf16[160,512]{1,0:T(8,128)(2,1)S(1)} %get-tuple-element.314), channel_id=1, source_target_pairs={{0,2},{1,3},{2,4},{3,5},{4,6},{5,7},{6,0},{7,1},{8,10},{9,11},{10,... | collective-permute-start | bytes 491528 | tf_op jit(solution)/shard_map/ppermute | solution.py:374
  11.7 11.2 %collective-permute-start.30 = (bf16[160,512]{1,0:T(8,128)(2,1)S(1)}, bf16[160,512]{1,0:T(8,128)(2,1)S(1)}, u32[]{:S(2)}, u32[]{:S(2)}) collective-permute-start(bf16[160,512]{1,0:T(8,128)(2,1)S(1)} %get-tuple-element.316), channel_id=1, source_target_pairs={{0,6},{1,7},{2,0},{3,1},{4,2},{5,3},{6,4},{7,5},{8,14},{9,15},{10,... | collective-permute-start | bytes 491528 | tf_op jit(solution)/shard_map/ppermute | solution.py:379
  16.1 26.0 %collective-permute-start.27 = (bf16[256,512]{1,0:T(8,128)(2,1)S(1)}, bf16[256,512]{1,0:T(8,128)(2,1)S(1)}, u32[]{:S(2)}, u32[]{:S(2)}) collective-permute-start(bf16[256,512]{1,0:T(8,128)(2,1)S(1)} %get-tuple-element.308), channel_id=1, source_target_pairs={{0,2},{1,3},{2,4},{3,5},{4,6},{5,7},{6,0},{7,1},{8,10},{9,11},{10,... | collective-permute-start | bytes 786440 | tf_op jit(solution)/shard_map/ppermute | solution.py:374
  17.5 24.6 %collective-permute-start.28 = (bf16[256,512]{1,0:T(8,128)(2,1)S(1)}, bf16[256,512]{1,0:T(8,128)(2,1)S(1)}, u32[]{:S(2)}, u32[]{:S(2)}) collective-permute-start(bf16[256,512]{1,0:T(8,128)(2,1)S(1)} %get-tuple-element.310), channel_id=1, source_target_pairs={{0,6},{1,7},{2,0},{3,1},{4,2},{5,3},{6,4},{7,5},{8,14},{9,15},{10,... | collective-permute-start | bytes 786440 | tf_op jit(solution)/shard_map/ppermute | solution.py:379
  22.9 12.3 %collective-permute-start.31 = (bf16[160,512]{1,0:T(8,128)(2,1)S(1)}, bf16[160,512]{1,0:T(8,128)(2,1)S(1)}, u32[]{:S(2)}, u32[]{:S(2)}) collective-permute-start(bf16[160,512]{1,0:T(8,128)(2,1)S(1)} %get-tuple-element.317), channel_id=1, source_target_pairs={{0,2},{1,3},{2,4},{3,5},{4,6},{5,7},{6,0},{7,1},{8,10},{9,11},{10,... | collective-permute-start | bytes 491528 | tf_op jit(solution)/shard_map/ppermute | solution.py:374
  25.3 16.8 %collective-permute-start.32 = (bf16[160,512]{1,0:T(8,128)(2,1)S(1)}, bf16[160,512]{1,0:T(8,128)(2,1)S(1)}, u32[]{:S(2)}, u32[]{:S(2)}) collective-permute-start(bf16[160,512]{1,0:T(8,128)(2,1)S(1)} %get-tuple-element.318), channel_id=1, source_target_pairs={{0,6},{1,7},{2,0},{3,1},{4,2},{5,3},{6,4},{7,5},{8,14},{9,15},{10,... | collective-permute-start | bytes 491528 | tf_op jit(solution)/shard_map/ppermute | solution.py:379
  43.4 21.7 %collective-permute-start.19 = (bf16[656,512]{1,0:T(8,128)(2,1)S(1)}, bf16[656,512]{1,0:T(8,128)(2,1)S(1)}, u32[]{:S(2)}, u32[]{:S(2)}) collective-permute-start(bf16[656,512]{1,0:T(8,128)(2,1)S(1)} %get-tuple-element.217), channel_id=1, source_target_pairs={{0,64},{8,72},{16,80},{24,88},{32,96},{40,104},{48,112},{56,120},{... | collective-permute-start | bytes 2015240 | tf_op jit(solution)/shard_map/cond/branch_3_fun/ppermute | solution.py:387
  46.1 11.2 %collective-permute-start.16 = (bf16[192,512]{1,0:T(8,128)(2,1)S(1)}, bf16[192,512]{1,0:T(8,128)(2,1)S(1)}, u32[]{:S(2)}, u32[]{:S(2)}) collective-permute-start(bf16[192,512]{1,0:T(8,128)(2,1)S(1)} %get-tuple-element.205), channel_id=1, source_target_pairs={{0,2},{1,3},{2,4},{3,5},{4,6},{5,7},{6,0},{7,1},{8,10},{9,11},{10,... | collective-permute-start | bytes 589832 | tf_op jit(solution)/shard_map/cond/branch_3_fun/ppermute | solution.py:374
  48.9 10.5 %collective-permute-start.17 = (bf16[192,512]{1,0:T(8,128)(2,1)S(1)}, bf16[192,512]{1,0:T(8,128)(2,1)S(1)}, u32[]{:S(2)}, u32[]{:S(2)}) collective-permute-start(bf16[192,512]{1,0:T(8,128)(2,1)S(1)} %get-tuple-element.206), channel_id=1, source_target_pairs={{0,6},{1,7},{2,0},{3,1},{4,2},{5,3},{6,4},{7,5},{8,14},{9,15},{10,... | collective-permute-start | bytes 589832 | tf_op jit(solution)/shard_map/cond/branch_3_fun/ppermute | solution.py:379
  61.5 12.3 %collective-permute-start.18 = (bf16[400,512]{1,0:T(8,128)(2,1)S(1)}, bf16[400,512]{1,0:T(8,128)(2,1)S(1)}, u32[]{:S(2)}, u32[]{:S(2)}) collective-permute-start(bf16[400,512]{1,0:T(8,128)(2,1)S(1)} %get-tuple-element.214), channel_id=1, source_target_pairs={{0,64},{8,72},{16,80},{24,88},{32,96},{40,104},{48,112},{56,120},{... | collective-permute-start | bytes 1228808 | tf_op jit(solution)/shard_map/cond/branch_3_fun/ppermute | solution.py:387
  62.3 13.2 %collective-permute-start.15 = (f32[1]{0:T(128)}, f32[1]{0:T(128)}, u32[]{:S(2)}, u32[]{:S(2)}) collective-permute-start(f32[1]{0:T(128)} %get-tuple-element.198.push_weight), channel_id=1, source_target_pairs={{0,64},{8,72},{16,80},{24,88},{32,96},{40,104},{48,112},{56,120},{... | collective-permute-start | bytes 20 | tf_op jit(solution)/shard_map/cond/branch_3_fun/ppermute | solution.py:387

commit v4 on v3

--- a/solution.py
+++ b/solution.py
@@ -88,27 +88,27 @@
     )(me, x, g)
 
 
-def others_kernel(me, x, g, out, far, near, x_held, sems):
+def column_blocks(me, x, other, held, sems, width):
+    groups = x.shape[1] // (2 * width)
+    return [
+        row_copies(x, pl.ds(first_column(me, ahead, other, width, groups), width), held.at[k], sems, PARTS * k)
+        for k, ahead in enumerate((1, -1, 0))
+    ]
+
+
+def others_kernel(me, x, g, out, far, x_held, sems):
     width = far.shape[1]
     groups = x.shape[1] // (2 * width)
-
-    def block(ahead, other, held, number):
-        low = first_column(me, ahead, other, width, groups)
-        return row_copies(x, pl.ds(low, width), held, sems, PARTS * number)
-
-    aheads = (1, -1, 0)
-    theirs = [block(ahead, True, x_held.at[k], k) for k, ahead in enumerate(aheads)]
-    own = [block(2, False, far, 3)] + [block(ahead, False, near.at[k], 4 + k) for k, ahead in enumerate(aheads)]
+    theirs = column_blocks(me, x, True, x_held, sems, width)
+    own = row_copies(x, pl.ds(first_column(me, 2, False, width, groups), width), far, sems, 3 * PARTS)
     start(theirs[0])
     start(theirs[1])
     for k in range(3):
         wait(theirs[k])
-        start(theirs[2] if k == 0 else own[0] if k == 1 else own[1])
+        if k < 2:
+            start((theirs[2], own)[k])
         out[pl.ds(k * width, width)] = product(x_held[k], g[...]).astype(BF16)
-    start(own[2])
-    start(own[3])
-    for copies in own:
-        wait(copies)
+    wait(own)
 
 
 def other_blocks(me, x, g, width):
@@ -116,9 +116,9 @@
     return pl.pallas_call(
         others_kernel,
         in_specs=[SMEM, HBM, VMEM],
-        out_specs=[VMEM] * 3,
-        out_shape=[shape(BF16, 3 * width, columns), shape(BF16, tokens, width), shape(BF16, 3, tokens, width)],
-        scratch_shapes=[pltpu.VMEM((3, tokens, width), BF16), pltpu.SemaphoreType.DMA((7 * PARTS,))],
+        out_specs=[VMEM] * 2,
+        out_shape=[shape(BF16, 3 * width, columns), shape(BF16, tokens, width)],
+        scratch_shapes=[pltpu.VMEM((3, tokens, width), BF16), pltpu.SemaphoreType.DMA((4 * PARTS,))],
         compiler_params=PARAMS,
         cost_estimate=SMALL,
         name="other_blocks",
@@ -146,14 +146,20 @@
     )(x, g, got)
 
 
-def near_kernel(x, g, got, far_up, far_down, *outs):
+def near_kernel(me, x, g, got, far_up, far_down, *outs):
+    *outs, x_held, sems = outs
     b_up, b_down, rest_up, rest_down, c_up_1, c_down_1, c_up_2, c_down_2, own_1, own_2 = outs
     width = got.shape[0] // 3
     (low_1, rows_1), (low_2, rows_2) = CHUNKS
     half_1, half_2 = rows_1 // 2, rows_2 // 2
 
+    blocks = column_blocks(me, x, False, x_held, sems, width)
+    for copies in blocks:
+        start(copies)
+
     def total(k):
-        return product(x[k], g[...]) + got[pl.ds(k * width, width)].astype(F32)
+        wait(blocks[k])
+        return product(x_held[k], g[...]) + got[pl.ds(k * width, width)].astype(F32)
 
     def plain(values, chunk_1, chunk_2, far, b, rest):
         b[:half_2] = far[...]
@@ -173,7 +179,7 @@
     own_2[...] = own[low_2 : low_2 + rows_2]
 
 
-def near_blocks(x, g, got, far_up, far_down):
+def near_blocks(me, x, g, got, far_up, far_down):
     columns = g.shape[1]
     (_, rows_1), (_, rows_2) = CHUNKS
     half_1, half_2 = rows_1 // 2, rows_2 // 2
@@ -182,13 +188,17 @@
     outs += [shape(F32, rows_1, columns), jax.ShapeDtypeStruct((rows_2, columns), F32)]
     return pl.pallas_call(
         near_kernel,
-        in_specs=[VMEM] * 5,
+        in_specs=[SMEM, HBM] + [VMEM] * 4,
         out_specs=[VMEM] * len(outs),
         out_shape=outs,
+        scratch_shapes=[
+            pltpu.VMEM((3, g.shape[0], got.shape[0] // 3), BF16),
+            pltpu.SemaphoreType.DMA((3 * PARTS,)),
+        ],
         compiler_params=PARAMS,
         cost_estimate=SMALL,
         name="near_blocks",
-    )(x, g, got, far_up, far_down)
+    )(me, x, g, got, far_up, far_down)
 
 
 def add_kernel(low, count, up, got_up, down, got_down, *rest):
@@ -419,12 +429,12 @@
     half_1, half_2 = rows_1 // 2, rows_2 // 2
     out_far, g_held = first_block(me, x, g, height)
     got_far = other_core(out_far)
-    out_near, x_far, x_near = other_blocks(me, x, g_held, height)
+    out_near, x_far = other_blocks(me, x, g_held, height)
     got_near = other_core(after(out_near, got_far))
     a_up_1, a_down_1, a_up_2, a_down_2 = far_block(x_far, g_held, got_far)
     got_a_up, got_a_down = up_z(a_up_1), down_z(a_down_1)
     b_up, b_down, *later, c_up_1, c_down_1, c_up_2, c_down_2, own_1, own_2 = near_blocks(
-        x_near, g_held, got_near, a_up_2, a_down_2
+        me, x, g_held, got_near, a_up_2, a_down_2
     )
     got_b = up_z(b_up), down_z(b_down)
     state_1 = fetch([(low_1, rows_1)] * 3, *(after(v, b_up) for v in state))

time: 77.8 us -> 73.9 us (0.950)
  waiting for transfers between devices: 29.1 us -> 25.3 us
  starting transfers between devices: 25 us -> 23.6 us
    ppermute x4, waiting for transfers between devices: 8.96 us -> 4.04 us  [down_z(): lax.ppermute(block, 'fsdp', [(i, (i - 2) % count) for i in range(count)])]
    ppermute x3, starting transfers between devices: 6.3 us -> 3.71 us  [from_partner(): lax.ppermute(block, 'rep', [(i, i ^ 1 << bit) for i in range(lax.axis_siz...]
    pallas_call x1, Pallas kernels: 2.18 us -> 3.91 us  [near_blocks(): pl.pallas_call(near_kernel, in_specs=[SMEM, HBM] + [VMEM] * 4, out_specs=...]
    ppermute x4, starting transfers between devices: 9.95 us -> 11.4 us  [up_z(): lax.ppermute(block, 'fsdp', [(i, (i + 2) % count) for i in range(count)])]
    pallas_call x1, Pallas kernels: 4.32 us -> 3.22 us  [other_blocks(): pl.pallas_call(others_kernel, in_specs=[SMEM, HBM, VMEM], out_specs=[VMEM...]
    ppermute x3, waiting for transfers between devices: 6.75 us -> 7.56 us  [from_partner(): lax.ppermute(block, 'rep', [(i, i ^ 1 << bit) for i in range(lax.axis_siz...]
  transfers between devices with their start and end apart: 13 -> 13, of which waited for: 6 -> 6; matrix products, arithmetic and copies ran while one was open for 0% -> 0% of each run, Pallas kernels for 21% -> 23%
where the time goes in v4:
time: 73.9 us; the launch traced here: 72.6 us
  waiting for transfers between devices  25.3 us (34%)
  starting transfers between devices  23.6 us (32%)
  Pallas kernels  19.6 us (27%)
  between operations  3.79 us (5%)
    ppermute x4, waiting for transfers between devices, up_z(): lax.ppermute(block, 'fsdp', [(i, (i + 2) % count) for i in range(count)])  13.7 us
    ppermute x4, starting transfers between devices, up_z(): lax.ppermute(block, 'fsdp', [(i, (i + 2) % count) for i in range(count)])  11.4 us
    ppermute x4, starting transfers between devices, down_z(): lax.ppermute(block, 'fsdp', [(i, (i - 2) % count) for i in range(count)])  7.78 us
    ppermute x3, waiting for transfers between devices, from_partner(): lax.ppermute(block, 'rep', [(i, i ^ 1 << bit) for i in range(lax.axis_siz...  7.56 us
    ppermute x4, waiting for transfers between devices, down_z(): lax.ppermute(block, 'fsdp', [(i, (i - 2) % count) for i in range(count)])  4.04 us
    pallas_call x1, Pallas kernels, near_blocks(): pl.pallas_call(near_kernel, in_specs=[SMEM, HBM] + [VMEM] * 4, out_specs=...  3.91 us
    ppermute x3, starting transfers between devices, from_partner(): lax.ppermute(block, 'rep', [(i, i ^ 1 << bit) for i in range(lax.axis_siz...  3.71 us
    pallas_call x2, Pallas kernels, mix_chunk(): pl.pallas_call(partial(mix_kernel, first_row, rows), in_specs=[SMEM] + [V...  3.54 us
  transfers between devices with their start and end apart: 13, of which 6 were waited for; matrix products, arithmetic and copies ran while one was open for 0% of the time, Pallas kernels for 23%

profile of v4, /device:TPU:56, one launch (start us, length us, event | category | flops | bytes accessed | tf_op | source)
XLA Modules:
  0.0 72.6 jit_solution(15171758906603949685)
XLA Ops:
  0.6 2.1 %first_block.1 = (bf16[512,512]{1,0:T(8,128)(2,1)S(1)}, bf16[704,512]{1,0:T(8,128)(2,1)S(1)}) custom-call(s32[1]{0:T(128)} %bitcast.4.me, bf16[704,4096]{1,0:T(8,128)(2,1)} %x.5, bf16[704,512]{1,0:T(8,128)(2,1)} %g.1), custom_call_target="tpu_custom_call" | custom-call | tf_op jit(solution)/shard_map/first_block/pallas_call | solution.py:79
  2.7 0.1 collective-permute-start.25
  2.8 3.2 %other_blocks.1 = (bf16[1536,512]{1,0:T(8,128)(2,1)S(1)}, bf16[704,512]{1,0:T(8,128)(2,1)S(1)}) custom-call(s32[1]{0:T(128)} %bitcast.4.me, bf16[704,4096]{1,0:T(8,128)(2,1)} %x.5, bf16[704,512]{1,0:T(8,128)(2,1)S(1)} %get-tuple-element.297.g), custom_call_target="tpu_custom_call" | custom-call | tf_op jit(solution)/shard_map/other_blocks/pallas_call | solution.py:116
  6.1 0.0 collective-permute-done.25.got
  6.1 0.6 collective-permute-start.26
  6.6 0.6 far_block.1
  7.2 3.3 %collective-permute-start.29 = (bf16[160,512]{1,0:T(8,128)(2,1)S(1)}, bf16[160,512]{1,0:T(8,128)(2,1)S(1)}, u32[]{:S(2)}, u32[]{:S(2)}) collective-permute-start(bf16[160,512]{1,0:T(8,128)(2,1)S(1)} %get-tuple-element.312), channel_id=1, source_target_pairs={{0,2},{1,3},{2,4},{3,5},{4,6},{5,7},{6,0},{7,1},{8,10},{9,11},{10,... | collective-permute-start | bytes 491528 | tf_op jit(solution)/shard_map/ppermute | solution.py:384
  10.6 2.2 %collective-permute-start.30 = (bf16[160,512]{1,0:T(8,128)(2,1)S(1)}, bf16[160,512]{1,0:T(8,128)(2,1)S(1)}, u32[]{:S(2)}, u32[]{:S(2)}) collective-permute-start(bf16[160,512]{1,0:T(8,128)(2,1)S(1)} %get-tuple-element.314), channel_id=1, source_target_pairs={{0,6},{1,7},{2,0},{3,1},{4,2},{5,3},{6,4},{7,5},{8,14},{9,15},{10,... | collective-permute-start | bytes 491528 | tf_op jit(solution)/shard_map/ppermute | solution.py:389
  12.8 0.0 collective-permute-done.26.got
  12.8 3.9 %near_blocks.1 = (bf16[256,512]{1,0:T(8,128)(2,1)S(1)}, bf16[256,512]{1,0:T(8,128)(2,1)S(1)}, bf16[96,512]{1,0:T(8,128)(2,1)S(1)}, bf16[96,512]{1,0:T(8,128)(2,1...) custom-call(s32[1]{0:T(128)} %bitcast.4.me, ...), custom_call_target="tpu_custom_call" | custom-call | tf_op jit(solution)/shard_map/near_blocks/pallas_call | solution.py:189
  16.7 1.4 %collective-permute-start.27 = (bf16[256,512]{1,0:T(8,128)(2,1)S(1)}, bf16[256,512]{1,0:T(8,128)(2,1)S(1)}, u32[]{:S(2)}, u32[]{:S(2)}) collective-permute-start(bf16[256,512]{1,0:T(8,128)(2,1)S(1)} %get-tuple-element.306), channel_id=1, source_target_pairs={{0,2},{1,3},{2,4},{3,5},{4,6},{5,7},{6,0},{7,1},{8,10},{9,11},{10,... | collective-permute-start | bytes 786440 | tf_op jit(solution)/shard_map/ppermute | solution.py:384
  18.2 2.8 %collective-permute-start.28 = (bf16[256,512]{1,0:T(8,128)(2,1)S(1)}, bf16[256,512]{1,0:T(8,128)(2,1)S(1)}, u32[]{:S(2)}, u32[]{:S(2)}) collective-permute-start(bf16[256,512]{1,0:T(8,128)(2,1)S(1)} %get-tuple-element.308), channel_id=1, source_target_pairs={{0,6},{1,7},{2,0},{3,1},{4,2},{5,3},{6,4},{7,5},{8,14},{9,15},{10,... | collective-permute-start | bytes 786440 | tf_op jit(solution)/shard_map/ppermute | solution.py:389
  21.0 0.0 collective-permute-done.29.got_up
  21.0 0.0 collective-permute-done.30.got_down
  21.0 0.1 add_far.2
  21.0 5.3 %collective-permute-start.31 = (bf16[160,512]{1,0:T(8,128)(2,1)S(1)}, bf16[160,512]{1,0:T(8,128)(2,1)S(1)}, u32[]{:S(2)}, u32[]{:S(2)}) collective-permute-start(bf16[160,512]{1,0:T(8,128)(2,1)S(1)} %get-tuple-element.315), channel_id=1, source_target_pairs={{0,2},{1,3},{2,4},{3,5},{4,6},{5,7},{6,0},{7,1},{8,10},{9,11},{10,... | collective-permute-start | bytes 491528 | tf_op jit(solution)/shard_map/ppermute | solution.py:384
  26.3 0.0 collective-permute-start.32
  27.6 1.5 %fetch.11 = (f32[320,512]{1,0:T(8,128)S(1)}, f32[320,512]{1,0:T(8,128)S(1)}, f32[320,512]{1,0:T(8,128)S(1)}) custom-call(f32[512,512]{1,0:T(8,128)} %bitcast.9, f32[512,512]{1,0:T(8,128)} %bitcast.15, f32[512,512]{1,0:T(8,128)} %bitcast.21), custom_call_target="tpu_custom_call" | custom-call | tf_op jit(solution)/shard_map/fetch/pallas_call | solution.py:244
  29.2 10.4 %collective-permute-done.31.rest_2_.c_up = bf16[160,512]{1,0:T(8,128)(2,1)S(1)} collective-permute-done((bf16[160,512]{1,0:T(8,128)(2,1)S(1)}, bf16[160,512]{1,0:T(8,128)(2,1)S(1)}, u32[]{:S(2)}, u32[]{:S(2)}) %collective-permute-start.31) | collective-permute-done | bytes 163872 | tf_op jit(solution)/shard_map/ppermute | solution.py:384
  39.5 2.5 %collective-permute-done.32.rest_3_.c_down = bf16[160,512]{1,0:T(8,128)(2,1)S(1)} collective-permute-done((bf16[160,512]{1,0:T(8,128)(2,1)S(1)}, bf16[160,512]{1,0:T(8,128)(2,1)S(1)}, u32[]{:S(2)}, u32[]{:S(2)}) %collective-permute-start.32) | collective-permute-done | bytes 163872 | tf_op jit(solution)/shard_map/ppermute | solution.py:389
  42.0 0.0 collective-permute-done.27.got_up.refs_0_
  42.0 0.0 collective-permute-done.28.got_down.refs_1_
  42.0 1.0 %step_chunk.11 = (f32[512,512]{1,0:T(8,128)}, f32[320,512]{1,0:T(8,128)S(1)}, f32[320,512]{1,0:T(8,128)S(1)}, bf16[656,512]{1,0:T(8,128)(2,1)S(1)}) custom-call(s32[1]{0:T(128)S(6)} %copy.86.step, f32[1]{0:T(128)S(6)} %copy.85.push_weight, f32[320,512]{1,0:T(8,128)S(1)} %get-tuple-element.323.own, bf16[160,512]{1,0:T(8,128)(2,1)S(1)} %collective-permute-done.31.rest_2_.c_up, ...), custom_call_target="tpu_custom_call" | custom-call | tf_op jit(solution)/shard_map/step_chunk/pallas_call | solution.py:304
  43.1 27.7 %conditional.1 = (f32[1]{0:T(128)}, f32[512,512]{1,0:T(8,128)}, f32[512,512]{1,0:T(8,128)}, f32[512,512]{1,0:T(8,128)}, bf16[512,512]{1,0:T(8,128)(2,1)}) conditional(s32[]{:T(128)} %bitcast, (f32[1]{0:T(128)}, f32[512,512]{1,0:T(8,128)}, f32[512,512]{1,0:T(8,128)}, f32[512,512]{1,0:T(8,128)}, f32[192,512]{1,0:T(8,128)}, ...), branch_computations={%region_0.0_spmd, %region_1.0_spmd, %region_2.0_spmd, %region_3.0_... | conditional | bytes 5898496 | solution.py:447
  43.3 1.6 %collective-permute-start.14 = (bf16[656,512]{1,0:T(8,128)(2,1)S(1)}, bf16[656,512]{1,0:T(8,128)(2,1)S(1)}, u32[]{:S(2)}, u32[]{:S(2)}) collective-permute-start(bf16[656,512]{1,0:T(8,128)(2,1)S(1)} %get-tuple-element.191), channel_id=1, source_target_pairs={{0,32},{8,40},{16,48},{24,56},{32,0},{40,8},{48,16},{56,24},{64,96... | collective-permute-start | bytes 2015240 | tf_op jit(solution)/shard_map/cond/branch_2_fun/ppermute | solution.py:397
  44.9 1.4 %collective-permute-start.11 = (bf16[192,512]{1,0:T(8,128)(2,1)S(1)}, bf16[192,512]{1,0:T(8,128)(2,1)S(1)}, u32[]{:S(2)}, u32[]{:S(2)}) collective-permute-start(bf16[192,512]{1,0:T(8,128)(2,1)S(1)} %get-tuple-element.179), channel_id=1, source_target_pairs={{0,2},{1,3},{2,4},{3,5},{4,6},{5,7},{6,0},{7,1},{8,10},{9,11},{10,... | collective-permute-start | bytes 589832 | tf_op jit(solution)/shard_map/cond/branch_2_fun/ppermute | solution.py:384
  46.3 2.8 %collective-permute-start.12 = (bf16[192,512]{1,0:T(8,128)(2,1)S(1)}, bf16[192,512]{1,0:T(8,128)(2,1)S(1)}, u32[]{:S(2)}, u32[]{:S(2)}) collective-permute-start(bf16[192,512]{1,0:T(8,128)(2,1)S(1)} %get-tuple-element.180), channel_id=1, source_target_pairs={{0,6},{1,7},{2,0},{3,1},{4,2},{5,3},{6,4},{7,5},{8,14},{9,15},{10,... | collective-permute-start | bytes 589832 | tf_op jit(solution)/shard_map/cond/branch_2_fun/ppermute | solution.py:389
  49.1 1.5 %fetch.8 = (f32[192,512]{1,0:T(8,128)S(1)}, f32[192,512]{1,0:T(8,128)S(1)}, f32[192,512]{1,0:T(8,128)S(1)}, f32[192,512]{1,0:T(8,128)S(1)}) custom-call(f32[512,512]{1,0:T(8,128)} %get-tuple-element.174.refs_0_, f32[512,512]{1,0:T(8,128)} %get-tuple-element.175.refs_1_, f32[512,512]{1,0:T(8,128)} %get-tuple-element.176.refs_2_, ...), custom_call_target="tpu_custom_call" | custom-call | tf_op jit(solution)/shard_map/cond/branch_2_fun/fetch/pallas_call | solution.py:244
  50.6 3.3 %collective-permute-done.11.c_up = bf16[192,512]{1,0:T(8,128)(2,1)S(1)} collective-permute-done((bf16[192,512]{1,0:T(8,128)(2,1)S(1)}, bf16[192,512]{1,0:T(8,128)(2,1)S(1)}, u32[]{:S(2)}, u32[]{:S(2)}) %collective-permute-start.11) | collective-permute-done | bytes 196640 | tf_op jit(solution)/shard_map/cond/branch_2_fun/ppermute | solution.py:384
  53.9 1.5 %collective-permute-done.12.c_down = bf16[192,512]{1,0:T(8,128)(2,1)S(1)} collective-permute-done((bf16[192,512]{1,0:T(8,128)(2,1)S(1)}, bf16[192,512]{1,0:T(8,128)(2,1)S(1)}, u32[]{:S(2)}, u32[]{:S(2)}) %collective-permute-start.12) | collective-permute-done | bytes 196640 | tf_op jit(solution)/shard_map/cond/branch_2_fun/ppermute | solution.py:389
  55.5 2.1 %step_chunk.8 = (f32[512,512]{1,0:T(8,128)}, f32[192,512]{1,0:T(8,128)S(1)}, f32[192,512]{1,0:T(8,128)S(1)}, bf16[400,512]{1,0:T(8,128)(2,1)S(1)}) custom-call(s32[1]{0:T(128)} %get-tuple-element.173.step, f32[1]{0:T(128)} %get-tuple-element.172.push_weight, f32[192,512]{1,0:T(8,128)S(1)} %get-tuple-element.178.own, ...), custom_call_target="tpu_custom_call", output_to_operand_aliasing={{0}: (8, {})} | custom-call | tf_op jit(solution)/shard_map/cond/branch_2_fun/step_chunk/pallas_call | solution.py:304
  57.6 0.6 collective-permute-start.13
  58.2 1.5 %collective-permute-start.10 = (f32[1]{0:T(128)}, f32[1]{0:T(128)}, u32[]{:S(2)}, u32[]{:S(2)}) collective-permute-start(f32[1]{0:T(128)} %get-tuple-element.172.push_weight), channel_id=1, source_target_pairs={{0,32},{8,40},{16,48},{24,56},{32,0},{40,8},{48,16},{56,24},{64,96... | collective-permute-start | bytes 20 | tf_op jit(solution)/shard_map/cond/branch_2_fun/ppermute | solution.py:397
  59.7 1.7 %collective-permute-done.14.got = bf16[656,512]{1,0:T(8,128)(2,1)S(1)} collective-permute-done((bf16[656,512]{1,0:T(8,128)(2,1)S(1)}, bf16[656,512]{1,0:T(8,128)(2,1)S(1)}, u32[]{:S(2)}, u32[]{:S(2)}) %collective-permute-start.14) | collective-permute-done | bytes 671776 | tf_op jit(solution)/shard_map/cond/branch_2_fun/ppermute | solution.py:397
  61.4 1.9 %mix_chunk.14 = (f32[512,512]{1,0:T(8,128)}, f32[512,512]{1,0:T(8,128)}, bf16[512,512]{1,0:T(8,128)(2,1)}) custom-call(f32[1]{0:T(128)} %get-tuple-element.172.push_weight, f32[320,512]{1,0:T(8,128)S(1)} %get-tuple-element.189.halfway, f32[320,512]{1,0:T(8,128)S(1)} %get-tuple-element.190.first, bf16[656,512]{1,0:T(8,128)(2,1)S(1)} %collective-permute-done.14.got), custom_call_target="tpu_custom_call" | custom-call | tf_op jit(solution)/shard_map/cond/branch_2_fun/mix_chunk/pallas_call | solution.py:346
  63.3 5.9 %collective-permute-done.13.got = bf16[400,512]{1,0:T(8,128)(2,1)S(1)} collective-permute-done((bf16[400,512]{1,0:T(8,128)(2,1)S(1)}, bf16[400,512]{1,0:T(8,128)(2,1)S(1)}, u32[]{:S(2)}, u32[]{:S(2)}) %collective-permute-start.13) | collective-permute-done | bytes 409632 | tf_op jit(solution)/shard_map/cond/branch_2_fun/ppermute | solution.py:397
  69.2 1.7 %mix_chunk.15 = (f32[512,512]{1,0:T(8,128)}, f32[512,512]{1,0:T(8,128)}, bf16[512,512]{1,0:T(8,128)(2,1)}) custom-call(f32[1]{0:T(128)} %get-tuple-element.172.push_weight, f32[192,512]{1,0:T(8,128)S(1)} %get-tuple-element.186.halfway, f32[192,512]{1,0:T(8,128)S(1)} %get-tuple-element.187.first, ...), custom_call_target="tpu_custom_call", output_to_operand_aliasing={{0}: (4, {}), {1}: (5, {}), {2}: (6, {})} | custom-call | tf_op jit(solution)/shard_map/cond/branch_2_fun/mix_chunk/pallas_call | solution.py:346
  70.8 0.0 collective-permute-done.10
  (2 shorter events, 0.1 us)
Async XLA Ops:
  2.7 3.3 %collective-permute-start.25 = (bf16[512,512]{1,0:T(8,128)(2,1)S(1)}, bf16[512,512]{1,0:T(8,128)(2,1)S(1)}, u32[]{:S(2)}, u32[]{:S(2)}) collective-permute-start(bf16[512,512]{1,0:T(8,128)(2,1)S(1)} %get-tuple-element.299), channel_id=1, source_target_pairs={{0,1},{1,0},{2,3},{3,2},{4,5},{5,4},{6,7},{7,6},{8,9},{9,8},{10,11... | collective-permute-start | bytes 1572872 | tf_op jit(solution)/shard_map/ppermute | solution.py:393
  6.1 6.7 %collective-permute-start.26 = (bf16[1536,512]{1,0:T(8,128)(2,1)S(1)}, bf16[1536,512]{1,0:T(8,128)(2,1)S(1)}, u32[]{:S(2)}, u32[]{:S(2)}) collective-permute-start(bf16[1536,512]{1,0:T(8,128)(2,1)S(1)} %get-tuple-element.300), channel_id=1, source_target_pairs={{0,1},{1,0},{2,3},{3,2},{4,5},{5,4},{6,7},{7,6},{8,9},{9,8},{10,11... | collective-permute-start | bytes 4718600 | tf_op jit(solution)/shard_map/ppermute | solution.py:393
  7.2 13.7 %collective-permute-start.29 = (bf16[160,512]{1,0:T(8,128)(2,1)S(1)}, bf16[160,512]{1,0:T(8,128)(2,1)S(1)}, u32[]{:S(2)}, u32[]{:S(2)}) collective-permute-start(bf16[160,512]{1,0:T(8,128)(2,1)S(1)} %get-tuple-element.312), channel_id=1, source_target_pairs={{0,2},{1,3},{2,4},{3,5},{4,6},{5,7},{6,0},{7,1},{8,10},{9,11},{10,... | collective-permute-start | bytes 491528 | tf_op jit(solution)/shard_map/ppermute | solution.py:384
  10.6 10.4 %collective-permute-start.30 = (bf16[160,512]{1,0:T(8,128)(2,1)S(1)}, bf16[160,512]{1,0:T(8,128)(2,1)S(1)}, u32[]{:S(2)}, u32[]{:S(2)}) collective-permute-start(bf16[160,512]{1,0:T(8,128)(2,1)S(1)} %get-tuple-element.314), channel_id=1, source_target_pairs={{0,6},{1,7},{2,0},{3,1},{4,2},{5,3},{6,4},{7,5},{8,14},{9,15},{10,... | collective-permute-start | bytes 491528 | tf_op jit(solution)/shard_map/ppermute | solution.py:389
  16.7 25.3 %collective-permute-start.27 = (bf16[256,512]{1,0:T(8,128)(2,1)S(1)}, bf16[256,512]{1,0:T(8,128)(2,1)S(1)}, u32[]{:S(2)}, u32[]{:S(2)}) collective-permute-start(bf16[256,512]{1,0:T(8,128)(2,1)S(1)} %get-tuple-element.306), channel_id=1, source_target_pairs={{0,2},{1,3},{2,4},{3,5},{4,6},{5,7},{6,0},{7,1},{8,10},{9,11},{10,... | collective-permute-start | bytes 786440 | tf_op jit(solution)/shard_map/ppermute | solution.py:384
  18.2 23.9 %collective-permute-start.28 = (bf16[256,512]{1,0:T(8,128)(2,1)S(1)}, bf16[256,512]{1,0:T(8,128)(2,1)S(1)}, u32[]{:S(2)}, u32[]{:S(2)}) collective-permute-start(bf16[256,512]{1,0:T(8,128)(2,1)S(1)} %get-tuple-element.308), channel_id=1, source_target_pairs={{0,6},{1,7},{2,0},{3,1},{4,2},{5,3},{6,4},{7,5},{8,14},{9,15},{10,... | collective-permute-start | bytes 786440 | tf_op jit(solution)/shard_map/ppermute | solution.py:389
  21.0 18.5 %collective-permute-start.31 = (bf16[160,512]{1,0:T(8,128)(2,1)S(1)}, bf16[160,512]{1,0:T(8,128)(2,1)S(1)}, u32[]{:S(2)}, u32[]{:S(2)}) collective-permute-start(bf16[160,512]{1,0:T(8,128)(2,1)S(1)} %get-tuple-element.315), channel_id=1, source_target_pairs={{0,2},{1,3},{2,4},{3,5},{4,6},{5,7},{6,0},{7,1},{8,10},{9,11},{10,... | collective-permute-start | bytes 491528 | tf_op jit(solution)/shard_map/ppermute | solution.py:384
  26.3 15.7 %collective-permute-start.32 = (bf16[160,512]{1,0:T(8,128)(2,1)S(1)}, bf16[160,512]{1,0:T(8,128)(2,1)S(1)}, u32[]{:S(2)}, u32[]{:S(2)}) collective-permute-start(bf16[160,512]{1,0:T(8,128)(2,1)S(1)} %get-tuple-element.316), channel_id=1, source_target_pairs={{0,6},{1,7},{2,0},{3,1},{4,2},{5,3},{6,4},{7,5},{8,14},{9,15},{10,... | collective-permute-start | bytes 491528 | tf_op jit(solution)/shard_map/ppermute | solution.py:389
  43.3 18.0 %collective-permute-start.14 = (bf16[656,512]{1,0:T(8,128)(2,1)S(1)}, bf16[656,512]{1,0:T(8,128)(2,1)S(1)}, u32[]{:S(2)}, u32[]{:S(2)}) collective-permute-start(bf16[656,512]{1,0:T(8,128)(2,1)S(1)} %get-tuple-element.191), channel_id=1, source_target_pairs={{0,32},{8,40},{16,48},{24,56},{32,0},{40,8},{48,16},{56,24},{64,96... | collective-permute-start | bytes 2015240 | tf_op jit(solution)/shard_map/cond/branch_2_fun/ppermute | solution.py:397
  44.9 9.0 %collective-permute-start.11 = (bf16[192,512]{1,0:T(8,128)(2,1)S(1)}, bf16[192,512]{1,0:T(8,128)(2,1)S(1)}, u32[]{:S(2)}, u32[]{:S(2)}) collective-permute-start(bf16[192,512]{1,0:T(8,128)(2,1)S(1)} %get-tuple-element.179), channel_id=1, source_target_pairs={{0,2},{1,3},{2,4},{3,5},{4,6},{5,7},{6,0},{7,1},{8,10},{9,11},{10,... | collective-permute-start | bytes 589832 | tf_op jit(solution)/shard_map/cond/branch_2_fun/ppermute | solution.py:384
  46.3 9.2 %collective-permute-start.12 = (bf16[192,512]{1,0:T(8,128)(2,1)S(1)}, bf16[192,512]{1,0:T(8,128)(2,1)S(1)}, u32[]{:S(2)}, u32[]{:S(2)}) collective-permute-start(bf16[192,512]{1,0:T(8,128)(2,1)S(1)} %get-tuple-element.180), channel_id=1, source_target_pairs={{0,6},{1,7},{2,0},{3,1},{4,2},{5,3},{6,4},{7,5},{8,14},{9,15},{10,... | collective-permute-start | bytes 589832 | tf_op jit(solution)/shard_map/cond/branch_2_fun/ppermute | solution.py:389
  57.6 11.6 %collective-permute-start.13 = (bf16[400,512]{1,0:T(8,128)(2,1)S(1)}, bf16[400,512]{1,0:T(8,128)(2,1)S(1)}, u32[]{:S(2)}, u32[]{:S(2)}) collective-permute-start(bf16[400,512]{1,0:T(8,128)(2,1)S(1)} %get-tuple-element.188), channel_id=1, source_target_pairs={{0,32},{8,40},{16,48},{24,56},{32,0},{40,8},{48,16},{56,24},{64,96... | collective-permute-start | bytes 1228808 | tf_op jit(solution)/shard_map/cond/branch_2_fun/ppermute | solution.py:397
  58.2 12.6 %collective-permute-start.10 = (f32[1]{0:T(128)}, f32[1]{0:T(128)}, u32[]{:S(2)}, u32[]{:S(2)}) collective-permute-start(f32[1]{0:T(128)} %get-tuple-element.172.push_weight), channel_id=1, source_target_pairs={{0,32},{8,40},{16,48},{24,56},{32,0},{40,8},{48,16},{56,24},{64,96... | collective-permute-start | bytes 20 | tf_op jit(solution)/shard_map/cond/branch_2_fun/ppermute | solution.py:397
